TPU v7x, 256 devices: a whole 4x4x8 slice. The times are simulated.
256 devices in a mesh: row: 32 (over z_hi, y, core), col: 8 (over x, z_lo).
Axes of the slice: x: 4, y: 4, z: 8 (z_hi: 4, z_lo: 2; z = z_hi * 2 + z_lo), core: 2. Of those that a mesh axis runs over, the one named last changes fastest.
Arguments:
- residues: int32 [1024], P('row'), may hold values from 0 to 20
- embed_table: bfloat16 [21, 256], replicated, may hold values from -6 to 6
- conv_first: bfloat16 [4352, 256], replicated, may hold values from -0.09375 to 0.09375
- conv_second: bfloat16 [4352, 256], replicated, may hold values from -0.09375 to 0.09375
- proj_row: bfloat16 [256, 64], replicated, may hold values from -0.375 to 0.375
- proj_col: bfloat16 [256, 64], replicated, may hold values from -0.375 to 0.375
- pair_weights: bfloat16 [4, 64, 576], replicated, may hold values from -0.25 to 0.25
Outputs:
- pair_out: bfloat16 [64, 1024, 1024], P(None, 'row', 'col')
All inputs are finite; a program needn't handle non-finite values.
Results may differ from a plain program's by a relative error of at most 0.018.
Values may be sent and summed in bfloat16 or wider, within the bound.
No kernel may reach another device: no remote copies, remote signals or barrier semaphores. Data moves between devices by JAX's collectives and lax.ppermute only.
A program may use at most 64 MiB of HBM per device.

v0:
```python
import jax
import jax.numpy as jnp
from jax import lax
from jax.sharding import PartitionSpec as P

KERNEL = 17
LAYERS = 4


def padded_2(shard, sides, width):
    for axis, dim in sides:
        size, length = (lax.axis_size(axis), shard.shape[dim])
        up = [(i, (i + 1) % size) for i in range(size - 1)]
        down = [(j, i) for i, j in up]
        last = lax.slice_in_dim(shard, length - width, length, axis=dim)
        leading = lax.slice_in_dim(shard, 0, width, axis=dim)
        before = lax.ppermute(last, axis, up)
        after = lax.ppermute(leading, axis, down)
        shard = jnp.concatenate([before, shard, after], axis=dim)
    return shard


def sent_to_all(shard, axis):
    copies = jnp.broadcast_to(shard, (lax.axis_size(axis), *shard.shape))
    return lax.all_to_all(copies, axis, split_axis=0, concat_axis=0, tiled=True)


def in_order(blocks, dim):
    blocks = jnp.moveaxis(blocks, 0, dim)
    shape = blocks.shape
    return blocks.reshape(*shape[:dim], shape[dim] * shape[dim + 1], *shape[dim + 2 :])


def collect(shard, axis, dim):
    blocks = sent_to_all(shard, axis)
    return in_order(blocks, dim)


def elu(v):
    return jnp.where(v > 0, v, jnp.expm1(jnp.minimum(v, 0.0)))


def conv_seq(feats, weight_stack):
    half = KERNEL // 2
    length = feats.shape[0]
    padded = padded_2(feats, (("row", 0),), half)
    windows = jnp.concatenate([padded[k : k + length] for k in range(KERNEL)], axis=1)
    return jnp.dot(windows, weight_stack, preferred_element_type=jnp.float32)


def offset_sum(weight_stack, activation_map, dilation_rate, row_span, column_span):
    chans = activation_map.shape[0]
    total = jnp.zeros((weight_stack.shape[0], row_span, column_span), jnp.float32)
    for offset_row in range(3):
        for offset_column in range(3):
            tap = 3 * offset_row + offset_column
            block = weight_stack[:, tap * chans : (tap + 1) * chans]
            window_extent = activation_map[
                :,
                offset_row * dilation_rate : offset_row * dilation_rate + row_span,
                offset_column * dilation_rate : offset_column * dilation_rate + column_span,
            ]
            total = total + jnp.einsum(
                "oc,cij->oij", block, window_extent, preferred_element_type=jnp.float32
            )
    return total


def apply_activation(pair_features):
    return elu(pair_features.astype(jnp.float32)).astype(jnp.bfloat16)


def layer_borders(pair_features, weight_stack, dilation_rate):
    activation_map = padded_2(
        apply_activation(pair_features), (("row", 1), ("col", 2)), dilation_rate
    )
    output_map = offset_sum(
        weight_stack, activation_map, dilation_rate, pair_features.shape[1], pair_features.shape[2]
    )
    return (pair_features.astype(jnp.float32) + output_map).astype(jnp.bfloat16)


def local(residues, embed_table, conv_first, conv_second, proj_row, proj_col, pair_weights):
    row_span = residues.shape[0]
    window_extent = row_span * lax.axis_size("row")
    tile = window_extent // lax.axis_size("col")
    col_start = lax.axis_index("col") * tile
    onehot = (
        residues[:, None] == jnp.arange(embed_table.shape[0], dtype=jnp.int32)[None, :]
    ).astype(jnp.bfloat16)
    embedded = jnp.dot(onehot, embed_table, preferred_element_type=jnp.float32).astype(jnp.bfloat16)
    first = elu(conv_seq(embedded, conv_first)).astype(jnp.bfloat16)
    second = (first.astype(jnp.float32) + elu(conv_seq(first, conv_second))).astype(jnp.bfloat16)
    left = jnp.dot(second, proj_row, preferred_element_type=jnp.float32).astype(jnp.bfloat16)
    local_right = jnp.dot(second, proj_col, preferred_element_type=jnp.float32).astype(jnp.bfloat16)
    every_right = collect(local_right, "row", 0)
    right = lax.dynamic_slice_in_dim(every_right, col_start, tile, 0)
    pair_features = (
        left.T.astype(jnp.float32)[:, :, None] + right.T.astype(jnp.float32)[:, None, :]
    ).astype(jnp.bfloat16)
    for layer_number in range(LAYERS):
        pair_features = layer_borders(pair_features, pair_weights[layer_number], 2**layer_number)
    return pair_features


def solution(mesh):
    return jax.shard_map(
        local,
        mesh=mesh,
        in_specs=(P("row"), P(), P(), P(), P(), P(), P()),
        out_specs=P(None, "row", "col"),
        check_vma=False,
    )
```

profile of v0, /device:TPU:91, one launch (start us, length us, event | category | flops | bytes accessed | tf_op | source)
XLA Modules:
  0.0 169.2 jit_solution(17041782426132856354)
XLA Ops:
  1.1 6.3 %collective-permute-start = (bf16[8,256]{1,0:T(8,128)(2,1)S(1)}, bf16[8,256]{1,0:T(8,128)(2,1)S(1)}, u32[]{:S(2)}, u32[]{:S(2)}) collective-permute-start(bf16[8,256]{1,0:T(8,128)(2,1)S(1)} %get-tuple-element.36), channel_id=1, source_target_pairs={{0,8},{8,16},{16,24},{24,32},{32,40},{40,48},{48,56},{56,64},{64,7... | collective-permute-start | bytes 12296 | tf_op jit(solution)/shard_map/ppermute | solution.py:17
  7.4 1.9 %collective-permute-start.1 = (bf16[8,256]{1,0:T(8,128)(2,1)S(1)}, bf16[8,256]{1,0:T(8,128)(2,1)S(1)}, u32[]{:S(2)}, u32[]{:S(2)}) collective-permute-start(bf16[8,256]{1,0:T(8,128)(2,1)S(1)} %get-tuple-element.35), channel_id=1, source_target_pairs={{8,0},{16,8},{24,16},{32,24},{40,32},{48,40},{56,48},{64,56},{72,6... | collective-permute-start | bytes 12296 | tf_op jit(solution)/shard_map/ppermute | solution.py:18
  9.5 7.1 %collective-permute-done.1 = bf16[8,256]{1,0:T(8,128)(2,1)S(1)} collective-permute-done((bf16[8,256]{1,0:T(8,128)(2,1)S(1)}, bf16[8,256]{1,0:T(8,128)(2,1)S(1)}, u32[]{:S(2)}, u32[]{:S(2)}) %collective-permute-start.1) | collective-permute-done | bytes 4128 | tf_op jit(solution)/shard_map/ppermute | solution.py:18
  17.2 2.1 %collective-permute-start.2 = (bf16[8,256]{1,0:T(8,128)(2,1)S(1)}, bf16[8,256]{1,0:T(8,128)(2,1)S(1)}, u32[]{:S(2)}, u32[]{:S(2)}) collective-permute-start(bf16[8,256]{1,0:T(8,128)(2,1)S(1)} %get-tuple-element.34), channel_id=1, source_target_pairs={{0,8},{8,16},{16,24},{24,32},{32,40},{40,48},{48,56},{56,64},{64,7... | collective-permute-start | bytes 12296 | tf_op jit(solution)/shard_map/ppermute | solution.py:17
  19.3 2.4 %collective-permute-start.3 = (bf16[8,256]{1,0:T(8,128)(2,1)S(1)}, bf16[8,256]{1,0:T(8,128)(2,1)S(1)}, u32[]{:S(2)}, u32[]{:S(2)}) collective-permute-start(bf16[8,256]{1,0:T(8,128)(2,1)S(1)} %get-tuple-element.33), channel_id=1, source_target_pairs={{8,0},{16,8},{24,16},{32,24},{40,32},{48,40},{56,48},{64,56},{72,6... | collective-permute-start | bytes 12296 | tf_op jit(solution)/shard_map/ppermute | solution.py:18
  21.9 6.6 %collective-permute-done.3 = bf16[8,256]{1,0:T(8,128)(2,1)S(1)} collective-permute-done((bf16[8,256]{1,0:T(8,128)(2,1)S(1)}, bf16[8,256]{1,0:T(8,128)(2,1)S(1)}, u32[]{:S(2)}, u32[]{:S(2)}) %collective-permute-start.3) | collective-permute-done | bytes 4128 | tf_op jit(solution)/shard_map/ppermute | solution.py:18
  30.2 6.2 %all-to-all-start = ((bf16[32,2,1024]{2,1,0:T(2,128)(2,1)}), bf16[32,2,1024]{2,1,0:T(2,128)(2,1)S(1)}, u32[]{:S(2)}, u32[]{:S(2)}) async-start(bf16[32,2,1024]{2,1,0:T(2,128)(2,1)} %reshape.43), calls=%async_computation | async-start | bytes 262144 | tf_op jit(solution)/shard_map/all_to_all | solution.py:25
  36.6 7.3 %all-to-all-done = bf16[32,2,1024]{2,1,0:T(2,128)(2,1)S(1)} async-done(((bf16[32,2,1024]{2,1,0:T(2,128)(2,1)}), bf16[32,2,1024]{2,1,0:T(2,128)(2,1)S(1)}, u32[]{:S(2)}, u32[]{:S(2)}) %all-to-all-start) | async-done | bytes 131104 | tf_op jit(solution)/shard_map/all_to_all | solution.py:25
  44.8 4.2 %collective-permute-start.4 = (bf16[64,1,128]{2,0,1:T(8,128)(2,1)S(1)}, bf16[64,1,128]{2,0,1:T(8,128)(2,1)S(1)}, u32[]{:S(2)}, u32[]{:S(2)}) collective-permute-start(bf16[64,1,128]{2,0,1:T(8,128)(2,1)S(1)} %get-tuple-element.27), channel_id=1, source_target_pairs={{0,8},{8,16},{16,24},{24,32},{32,40},{40,48},{48,56},{56,64},{64,7... | collective-permute-start | bytes 49160 | tf_op jit(solution)/shard_map/ppermute | solution.py:17
  49.0 1.9 %collective-permute-start.5 = (bf16[64,1,128]{2,0,1:T(8,128)(2,1)S(1)}, bf16[64,1,128]{2,0,1:T(8,128)(2,1)S(1)}, u32[]{:S(2)}, u32[]{:S(2)}) collective-permute-start(bf16[64,1,128]{2,0,1:T(8,128)(2,1)S(1)} %get-tuple-element.28), channel_id=1, source_target_pairs={{8,0},{16,8},{24,16},{32,24},{40,32},{48,40},{56,48},{64,56},{72,6... | collective-permute-start | bytes 49160 | tf_op jit(solution)/shard_map/ppermute | solution.py:18
  51.6 6.7 %collective-permute-done.5 = bf16[64,1,128]{2,0,1:T(8,128)(2,1)S(1)} collective-permute-done((bf16[64,1,128]{2,0,1:T(8,128)(2,1)S(1)}, bf16[64,1,128]{2,0,1:T(8,128)(2,1)S(1)}, u32[]{:S(2)}, u32[]{:S(2)}) %collective-permute-start.5) | collective-permute-done | bytes 16416 | tf_op jit(solution)/shard_map/ppermute | solution.py:18
  58.9 2.8 %collective-permute-start.6 = (bf16[64,34,1]{0,1,2:T(8,128)(2,1)S(1)}, bf16[64,34,1]{0,1,2:T(8,128)(2,1)S(1)}, u32[]{:S(2)}, u32[]{:S(2)}) collective-permute-start(bf16[64,34,1]{0,1,2:T(8,128)(2,1)S(1)} %copy.13), channel_id=1, source_target_pairs={{0,1},{1,2},{2,3},{3,4},{4,5},{5,6},{6,7},{8,9},{9,10},{10,11},{11... | collective-permute-start | bytes 13064 | tf_op jit(solution)/shard_map/ppermute | solution.py:17
  62.1 3.3 %collective-permute-start.7 = (bf16[64,34,1]{0,1,2:T(8,128)(2,1)S(1)}, bf16[64,34,1]{0,1,2:T(8,128)(2,1)S(1)}, u32[]{:S(2)}, u32[]{:S(2)}) collective-permute-start(bf16[64,34,1]{0,1,2:T(8,128)(2,1)S(1)} %copy.15), channel_id=1, source_target_pairs={{1,0},{2,1},{3,2},{4,3},{5,4},{6,5},{7,6},{9,8},{10,9},{11,10},{12... | collective-permute-start | bytes 13064 | tf_op jit(solution)/shard_map/ppermute | solution.py:18
  73.5 2.8 %collective-permute-start.8 = (bf16[64,2,128]{2,0,1:T(8,128)(2,1)S(1)}, bf16[64,2,128]{2,0,1:T(8,128)(2,1)S(1)}, u32[]{:S(2)}, u32[]{:S(2)}) collective-permute-start(bf16[64,2,128]{2,0,1:T(8,128)(2,1)S(1)} %get-tuple-element.25), channel_id=1, source_target_pairs={{0,8},{8,16},{16,24},{24,32},{32,40},{40,48},{48,56},{56,64},{64,7... | collective-permute-start | bytes 98312 | tf_op jit(solution)/shard_map/ppermute | solution.py:17
  76.3 1.9 %collective-permute-start.9 = (bf16[64,2,128]{2,0,1:T(8,128)(2,1)S(1)}, bf16[64,2,128]{2,0,1:T(8,128)(2,1)S(1)}, u32[]{:S(2)}, u32[]{:S(2)}) collective-permute-start(bf16[64,2,128]{2,0,1:T(8,128)(2,1)S(1)} %get-tuple-element.26), channel_id=1, source_target_pairs={{8,0},{16,8},{24,16},{32,24},{40,32},{48,40},{56,48},{64,56},{72,6... | collective-permute-start | bytes 98312 | tf_op jit(solution)/shard_map/ppermute | solution.py:18
  78.2 7.6 %collective-permute-done.9 = bf16[64,2,128]{2,0,1:T(8,128)(2,1)S(1)} collective-permute-done((bf16[64,2,128]{2,0,1:T(8,128)(2,1)S(1)}, bf16[64,2,128]{2,0,1:T(8,128)(2,1)S(1)}, u32[]{:S(2)}, u32[]{:S(2)}) %collective-permute-start.9) | collective-permute-done | bytes 32800 | tf_op jit(solution)/shard_map/ppermute | solution.py:18
  86.5 4.4 %collective-permute-start.10 = (bf16[64,36,2]{0,2,1:T(2,128)(2,1)S(1)}, bf16[64,36,2]{0,2,1:T(2,128)(2,1)S(1)}, u32[]{:S(2)}, u32[]{:S(2)}) collective-permute-start(bf16[64,36,2]{0,2,1:T(2,128)(2,1)S(1)} %copy.17), channel_id=1, source_target_pairs={{0,1},{1,2},{2,3},{3,4},{4,5},{5,6},{6,7},{8,9},{9,10},{10,11},{11... | collective-permute-start | bytes 27656 | tf_op jit(solution)/shard_map/ppermute | solution.py:17
  91.1 2.1 %collective-permute-start.11 = (bf16[64,36,2]{0,2,1:T(2,128)(2,1)S(1)}, bf16[64,36,2]{0,2,1:T(2,128)(2,1)S(1)}, u32[]{:S(2)}, u32[]{:S(2)}) collective-permute-start(bf16[64,36,2]{0,2,1:T(2,128)(2,1)S(1)} %copy.19), channel_id=1, source_target_pairs={{1,0},{2,1},{3,2},{4,3},{5,4},{6,5},{7,6},{9,8},{10,9},{11,10},{12... | collective-permute-start | bytes 27656 | tf_op jit(solution)/shard_map/ppermute | solution.py:18
  102.2 3.3 %collective-permute-start.12 = (bf16[64,4,128]{2,0,1:T(8,128)(2,1)S(1)}, bf16[64,4,128]{2,0,1:T(8,128)(2,1)S(1)}, u32[]{:S(2)}, u32[]{:S(2)}) collective-permute-start(bf16[64,4,128]{2,0,1:T(8,128)(2,1)S(1)} %get-tuple-element.23), channel_id=1, source_target_pairs={{0,8},{8,16},{16,24},{24,32},{32,40},{40,48},{48,56},{56,64},{64,7... | collective-permute-start | bytes 196616 | tf_op jit(solution)/shard_map/ppermute | solution.py:17
  105.5 1.9 %collective-permute-start.13 = (bf16[64,4,128]{2,0,1:T(8,128)(2,1)S(1)}, bf16[64,4,128]{2,0,1:T(8,128)(2,1)S(1)}, u32[]{:S(2)}, u32[]{:S(2)}) collective-permute-start(bf16[64,4,128]{2,0,1:T(8,128)(2,1)S(1)} %get-tuple-element.24), channel_id=1, source_target_pairs={{8,0},{16,8},{24,16},{32,24},{40,32},{48,40},{56,48},{64,56},{72,6... | collective-permute-start | bytes 196616 | tf_op jit(solution)/shard_map/ppermute | solution.py:18
  107.5 8.6 %collective-permute-done.13 = bf16[64,4,128]{2,0,1:T(8,128)(2,1)S(1)} collective-permute-done((bf16[64,4,128]{2,0,1:T(8,128)(2,1)S(1)}, bf16[64,4,128]{2,0,1:T(8,128)(2,1)S(1)}, u32[]{:S(2)}, u32[]{:S(2)}) %collective-permute-start.13) | collective-permute-done | bytes 65568 | tf_op jit(solution)/shard_map/ppermute | solution.py:18
  117.0 2.1 %collective-permute-start.14 = (bf16[64,40,4]{0,1,2:T(8,128)(2,1)S(1)}, bf16[64,40,4]{0,1,2:T(8,128)(2,1)S(1)}, u32[]{:S(2)}, u32[]{:S(2)}) collective-permute-start(bf16[64,40,4]{0,1,2:T(8,128)(2,1)S(1)} %copy.21), channel_id=1, source_target_pairs={{0,1},{1,2},{2,3},{3,4},{4,5},{5,6},{6,7},{8,9},{9,10},{10,11},{11... | collective-permute-start | bytes 61448 | tf_op jit(solution)/shard_map/ppermute | solution.py:17
  119.4 4.1 %collective-permute-start.15 = (bf16[64,40,4]{0,1,2:T(8,128)(2,1)S(1)}, bf16[64,40,4]{0,1,2:T(8,128)(2,1)}, u32[]{:S(2)}, u32[]{:S(2)}) collective-permute-start(bf16[64,40,4]{0,1,2:T(8,128)(2,1)S(1)} %copy.23), channel_id=1, source_target_pairs={{1,0},{2,1},{3,2},{4,3},{5,4},{6,5},{7,6},{9,8},{10,9},{11,10},{12... | collective-permute-start | bytes 61448 | tf_op jit(solution)/shard_map/ppermute | solution.py:18
  125.9 2.2 %maximum_maximum_fusion.1 = (bf16[64,40,132]{2,0,1:T(8,128)(2,1)S(1)}, bf16[64,40,132]{2,0,1:T(8,128)(2,1)S(1)}) fusion(bf16[64,4,128]{2,0,1:T(8,128)(2,1)} %copy-done.8, bf16[64,32,128]{2,0,1:T(8,128)(2,1)S(1)} %get-tuple-element.39, bf16[64,4,128]{2,0,1:T(8,128)(2,1)} %copy-done.10, bf16[64,40,4]{2,0,1:T(8,128)(2,1)S(1)} %copy.22, ...), kind=kLoop, calls=%fused_computation.50 | loop fusion | flops 5406720 | bytes 2048000 | tf_op jit(solution)/shard_map/concatenate | solution.py:19
  132.2 2.7 %collective-permute-start.16 = (bf16[64,8,128]{2,0,1:T(8,128)(2,1)S(1)}, bf16[64,8,128]{2,0,1:T(8,128)(2,1)S(1)}, u32[]{:S(2)}, u32[]{:S(2)}) collective-permute-start(bf16[64,8,128]{2,0,1:T(8,128)(2,1)S(1)} %get-tuple-element.21), channel_id=1, source_target_pairs={{0,8},{8,16},{16,24},{24,32},{32,40},{40,48},{48,56},{56,64},{64,7... | collective-permute-start | bytes 393224 | tf_op jit(solution)/shard_map/ppermute | solution.py:17
  134.9 1.9 %collective-permute-start.17 = (bf16[64,8,128]{2,0,1:T(8,128)(2,1)S(1)}, bf16[64,8,128]{2,0,1:T(8,128)(2,1)S(1)}, u32[]{:S(2)}, u32[]{:S(2)}) collective-permute-start(bf16[64,8,128]{2,0,1:T(8,128)(2,1)S(1)} %get-tuple-element.22), channel_id=1, source_target_pairs={{8,0},{16,8},{24,16},{32,24},{40,32},{48,40},{56,48},{64,56},{72,6... | collective-permute-start | bytes 393224 | tf_op jit(solution)/shard_map/ppermute | solution.py:18
  138.3 7.3 %collective-permute-done.17 = bf16[64,8,128]{2,0,1:T(8,128)(2,1)S(1)} collective-permute-done((bf16[64,8,128]{2,0,1:T(8,128)(2,1)S(1)}, bf16[64,8,128]{2,0,1:T(8,128)(2,1)S(1)}, u32[]{:S(2)}, u32[]{:S(2)}) %collective-permute-start.17) | collective-permute-done | bytes 131104 | tf_op jit(solution)/shard_map/ppermute | solution.py:18
  148.3 5.1 %collective-permute-start.18 = (bf16[64,48,8]{0,2,1:T(8,128)(2,1)S(1)}, bf16[64,48,8]{0,2,1:T(8,128)(2,1)S(1)}, u32[]{:S(2)}, u32[]{:S(2)}) collective-permute-start(bf16[64,48,8]{0,2,1:T(8,128)(2,1)S(1)} %copy.25), channel_id=1, source_target_pairs={{0,1},{1,2},{2,3},{3,4},{4,5},{5,6},{6,7},{8,9},{9,10},{10,11},{11... | collective-permute-start | bytes 147464 | tf_op jit(solution)/shard_map/ppermute | solution.py:17
  153.7 2.4 %collective-permute-start.19 = (bf16[64,48,8]{0,2,1:T(8,128)(2,1)S(1)}, bf16[64,48,8]{0,2,1:T(8,128)(2,1)S(1)}, u32[]{:S(2)}, u32[]{:S(2)}) collective-permute-start(bf16[64,48,8]{0,2,1:T(8,128)(2,1)S(1)} %copy.27), channel_id=1, source_target_pairs={{1,0},{2,1},{3,2},{4,3},{5,4},{6,5},{7,6},{9,8},{10,9},{11,10},{12... | collective-permute-start | bytes 147464 | tf_op jit(solution)/shard_map/ppermute | solution.py:18
  156.1 2.0 %fusion.38 = f32[32,128,64]{1,2,0:T(8,128)} fusion(bf16[64,32,128]{2,0,1:T(8,128)(2,1)S(1)} %get-tuple-element.41, bf16[64,8,128]{2,0,1:T(8,128)(2,1)S(1)} %collective-permute-done.16, bf16[64,576]{1,0:T(8,128)(2,1)} %get-tuple-element.29), kind=kOutput, calls=%fused_computation.91 | convolution fusion | flops 34603008 | bytes 1720320 | tf_op jit(solution)/shard_map/oc,cij->oij/dot_general | solution.py:63
  158.1 2.1 %fusion.29 = f32[32,128,64]{1,2,0:T(8,128)} fusion(bf16[64,8,128]{2,0,1:T(8,128)(2,1)S(1)} %collective-permute-done.17, bf16[64,32,128]{2,0,1:T(8,128)(2,1)S(1)} %get-tuple-element.41, bf16[64,576]{1,0:T(8,128)(2,1)} %get-tuple-element.29), kind=kOutput, calls=%fused_computation.81 | convolution fusion | flops 34603008 | bytes 1720320 | tf_op jit(solution)/shard_map/oc,cij->oij/dot_general | solution.py:63
  161.7 2.7 %maximum_maximum_fusion = (bf16[64,48,136]{2,0,1:T(8,128)(2,1)S(1)}, bf16[64,48,136]{2,0,1:T(8,128)(2,1)S(1)}) fusion(bf16[64,8,128]{2,0,1:T(8,128)(2,1)S(1)} %collective-permute-done.17, bf16[64,32,128]{2,0,1:T(8,128)(2,1)S(1)} %get-tuple-element.41, bf16[64,8,128]{2,0,1:T(8,128)(2,1)S(1)} %collective-permute-done.16, bf16[64,48,8]{2,0,1:T(8,128)(2,1)S(1)} %copy.26, ...), kind=kLoop, calls=%fused_computation.4 | loop fusion | flops 6684672 | bytes 2555904 | tf_op jit(solution)/shard_map/concatenate | solution.py:19
  (157 shorter events, 42.3 us)
Async XLA Ops:
  0.0 16.7 %copy-start = (bf16[4352,256]{1,0:T(8,128)(2,1)S(1)}, bf16[4352,256]{1,0:T(8,128)(2,1)}, u32[]{:S(2)}) copy-start(bf16[4352,256]{1,0:T(8,128)(2,1)} %param.9) | copy-start | bytes 6684676
  1.1 8.3 %collective-permute-start = (bf16[8,256]{1,0:T(8,128)(2,1)S(1)}, bf16[8,256]{1,0:T(8,128)(2,1)S(1)}, u32[]{:S(2)}, u32[]{:S(2)}) collective-permute-start(bf16[8,256]{1,0:T(8,128)(2,1)S(1)} %get-tuple-element.36), channel_id=1, source_target_pairs={{0,8},{8,16},{16,24},{24,32},{32,40},{40,48},{48,56},{56,64},{64,7... | collective-permute-start | bytes 12296 | tf_op jit(solution)/shard_map/ppermute | solution.py:17
  7.4 9.1 %collective-permute-start.1 = (bf16[8,256]{1,0:T(8,128)(2,1)S(1)}, bf16[8,256]{1,0:T(8,128)(2,1)S(1)}, u32[]{:S(2)}, u32[]{:S(2)}) collective-permute-start(bf16[8,256]{1,0:T(8,128)(2,1)S(1)} %get-tuple-element.35), channel_id=1, source_target_pairs={{8,0},{16,8},{24,16},{32,24},{40,32},{48,40},{56,48},{64,56},{72,6... | collective-permute-start | bytes 12296 | tf_op jit(solution)/shard_map/ppermute | solution.py:18
  16.7 11.9 %copy-start.4 = (bf16[4352,256]{1,0:T(8,128)(2,1)S(1)}, bf16[4352,256]{1,0:T(8,128)(2,1)}, u32[]{:S(2)}) copy-start(bf16[4352,256]{1,0:T(8,128)(2,1)} %param.10) | copy-start | bytes 6684676
  17.2 4.5 %collective-permute-start.2 = (bf16[8,256]{1,0:T(8,128)(2,1)S(1)}, bf16[8,256]{1,0:T(8,128)(2,1)S(1)}, u32[]{:S(2)}, u32[]{:S(2)}) collective-permute-start(bf16[8,256]{1,0:T(8,128)(2,1)S(1)} %get-tuple-element.34), channel_id=1, source_target_pairs={{0,8},{8,16},{16,24},{24,32},{32,40},{40,48},{48,56},{56,64},{64,7... | collective-permute-start | bytes 12296 | tf_op jit(solution)/shard_map/ppermute | solution.py:17
  19.3 9.8 %copy-start.14 = (bf16[256,64]{0,1:T(8,128)(2,1)S(1)}, bf16[256,64]{0,1:T(8,128)(2,1)}, u32[]{:S(2)}) copy-start(bf16[256,64]{0,1:T(8,128)(2,1)} %param.12) | copy-start | bytes 98308
  19.3 9.1 %collective-permute-start.3 = (bf16[8,256]{1,0:T(8,128)(2,1)S(1)}, bf16[8,256]{1,0:T(8,128)(2,1)S(1)}, u32[]{:S(2)}, u32[]{:S(2)}) collective-permute-start(bf16[8,256]{1,0:T(8,128)(2,1)S(1)} %get-tuple-element.33), channel_id=1, source_target_pairs={{8,0},{16,8},{24,16},{32,24},{40,32},{48,40},{56,48},{64,56},{72,6... | collective-permute-start | bytes 12296 | tf_op jit(solution)/shard_map/ppermute | solution.py:18
  28.6 7.8 %copy-start.13 = (bf16[256,64]{0,1:T(8,128)(2,1)S(1)}, bf16[256,64]{0,1:T(8,128)(2,1)}, u32[]{:S(2)}) copy-start(bf16[256,64]{0,1:T(8,128)(2,1)} %param.11) | copy-start | bytes 98308
  29.1 21.8 %copy-start.11 = (bf16[4,64,576]{2,1,0:T(8,128)(2,1)S(1)}, bf16[4,64,576]{2,1,0:T(8,128)(2,1)}, u32[]{:S(2)}) copy-start(bf16[4,64,576]{2,1,0:T(8,128)(2,1)} %param.13) | copy-start | bytes 884740
  30.2 13.7 %all-to-all-start = ((bf16[32,2,1024]{2,1,0:T(2,128)(2,1)}), bf16[32,2,1024]{2,1,0:T(2,128)(2,1)S(1)}, u32[]{:S(2)}, u32[]{:S(2)}) async-start(bf16[32,2,1024]{2,1,0:T(2,128)(2,1)} %reshape.43), calls=%async_computation | async-start | bytes 262144 | tf_op jit(solution)/shard_map/all_to_all | solution.py:25
  44.8 6.8 %collective-permute-start.4 = (bf16[64,1,128]{2,0,1:T(8,128)(2,1)S(1)}, bf16[64,1,128]{2,0,1:T(8,128)(2,1)S(1)}, u32[]{:S(2)}, u32[]{:S(2)}) collective-permute-start(bf16[64,1,128]{2,0,1:T(8,128)(2,1)S(1)} %get-tuple-element.27), channel_id=1, source_target_pairs={{0,8},{8,16},{16,24},{24,32},{32,40},{40,48},{48,56},{56,64},{64,7... | collective-permute-start | bytes 49160 | tf_op jit(solution)/shard_map/ppermute | solution.py:17
  49.0 9.3 %collective-permute-start.5 = (bf16[64,1,128]{2,0,1:T(8,128)(2,1)S(1)}, bf16[64,1,128]{2,0,1:T(8,128)(2,1)S(1)}, u32[]{:S(2)}, u32[]{:S(2)}) collective-permute-start(bf16[64,1,128]{2,0,1:T(8,128)(2,1)S(1)} %get-tuple-element.28), channel_id=1, source_target_pairs={{8,0},{16,8},{24,16},{32,24},{40,32},{48,40},{56,48},{64,56},{72,6... | collective-permute-start | bytes 49160 | tf_op jit(solution)/shard_map/ppermute | solution.py:18
  51.6 72.0 %copy-start.6 = (bf16[64,576]{1,0:T(8,128)(2,1)}, bf16[64,576]{1,0:T(8,128)(2,1)S(1)}, u32[]{:S(2)}) copy-start(bf16[64,576]{1,0:T(8,128)(2,1)S(1)} %get-tuple-element.32) | copy-start | bytes 221188
  51.6 7.0 %copy-start.12 = (bf16[64,1,128]{2,0,1:T(8,128)(2,1)}, bf16[64,1,128]{2,0,1:T(8,128)(2,1)S(1)}, u32[]{:S(2)}) copy-start(bf16[64,1,128]{2,0,1:T(8,128)(2,1)S(1)} %collective-permute-done.4) | copy-start | bytes 49156
  58.9 7.6 %collective-permute-start.6 = (bf16[64,34,1]{0,1,2:T(8,128)(2,1)S(1)}, bf16[64,34,1]{0,1,2:T(8,128)(2,1)S(1)}, u32[]{:S(2)}, u32[]{:S(2)}) collective-permute-start(bf16[64,34,1]{0,1,2:T(8,128)(2,1)S(1)} %copy.13), channel_id=1, source_target_pairs={{0,1},{1,2},{2,3},{3,4},{4,5},{5,6},{6,7},{8,9},{9,10},{10,11},{11... | collective-permute-start | bytes 13064 | tf_op jit(solution)/shard_map/ppermute | solution.py:17
  62.1 4.8 %collective-permute-start.7 = (bf16[64,34,1]{0,1,2:T(8,128)(2,1)S(1)}, bf16[64,34,1]{0,1,2:T(8,128)(2,1)S(1)}, u32[]{:S(2)}, u32[]{:S(2)}) collective-permute-start(bf16[64,34,1]{0,1,2:T(8,128)(2,1)S(1)} %copy.15), channel_id=1, source_target_pairs={{1,0},{2,1},{3,2},{4,3},{5,4},{6,5},{7,6},{9,8},{10,9},{11,10},{12... | collective-permute-start | bytes 13064 | tf_op jit(solution)/shard_map/ppermute | solution.py:18
  73.5 4.7 %collective-permute-start.8 = (bf16[64,2,128]{2,0,1:T(8,128)(2,1)S(1)}, bf16[64,2,128]{2,0,1:T(8,128)(2,1)S(1)}, u32[]{:S(2)}, u32[]{:S(2)}) collective-permute-start(bf16[64,2,128]{2,0,1:T(8,128)(2,1)S(1)} %get-tuple-element.25), channel_id=1, source_target_pairs={{0,8},{8,16},{16,24},{24,32},{32,40},{40,48},{48,56},{56,64},{64,7... | collective-permute-start | bytes 98312 | tf_op jit(solution)/shard_map/ppermute | solution.py:17
  76.3 9.6 %collective-permute-start.9 = (bf16[64,2,128]{2,0,1:T(8,128)(2,1)S(1)}, bf16[64,2,128]{2,0,1:T(8,128)(2,1)S(1)}, u32[]{:S(2)}, u32[]{:S(2)}) collective-permute-start(bf16[64,2,128]{2,0,1:T(8,128)(2,1)S(1)} %get-tuple-element.26), channel_id=1, source_target_pairs={{8,0},{16,8},{24,16},{32,24},{40,32},{48,40},{56,48},{64,56},{72,6... | collective-permute-start | bytes 98312 | tf_op jit(solution)/shard_map/ppermute | solution.py:18
  86.5 7.1 %collective-permute-start.10 = (bf16[64,36,2]{0,2,1:T(2,128)(2,1)S(1)}, bf16[64,36,2]{0,2,1:T(2,128)(2,1)S(1)}, u32[]{:S(2)}, u32[]{:S(2)}) collective-permute-start(bf16[64,36,2]{0,2,1:T(2,128)(2,1)S(1)} %copy.17), channel_id=1, source_target_pairs={{0,1},{1,2},{2,3},{3,4},{4,5},{5,6},{6,7},{8,9},{9,10},{10,11},{11... | collective-permute-start | bytes 27656 | tf_op jit(solution)/shard_map/ppermute | solution.py:17
  91.1 4.5 %collective-permute-start.11 = (bf16[64,36,2]{0,2,1:T(2,128)(2,1)S(1)}, bf16[64,36,2]{0,2,1:T(2,128)(2,1)S(1)}, u32[]{:S(2)}, u32[]{:S(2)}) collective-permute-start(bf16[64,36,2]{0,2,1:T(2,128)(2,1)S(1)} %copy.19), channel_id=1, source_target_pairs={{1,0},{2,1},{3,2},{4,3},{5,4},{6,5},{7,6},{9,8},{10,9},{11,10},{12... | collective-permute-start | bytes 27656 | tf_op jit(solution)/shard_map/ppermute | solution.py:18
  102.2 5.3 %collective-permute-start.12 = (bf16[64,4,128]{2,0,1:T(8,128)(2,1)S(1)}, bf16[64,4,128]{2,0,1:T(8,128)(2,1)S(1)}, u32[]{:S(2)}, u32[]{:S(2)}) collective-permute-start(bf16[64,4,128]{2,0,1:T(8,128)(2,1)S(1)} %get-tuple-element.23), channel_id=1, source_target_pairs={{0,8},{8,16},{16,24},{24,32},{32,40},{40,48},{48,56},{56,64},{64,7... | collective-permute-start | bytes 196616 | tf_op jit(solution)/shard_map/ppermute | solution.py:17
  105.5 10.5 %collective-permute-start.13 = (bf16[64,4,128]{2,0,1:T(8,128)(2,1)S(1)}, bf16[64,4,128]{2,0,1:T(8,128)(2,1)S(1)}, u32[]{:S(2)}, u32[]{:S(2)}) collective-permute-start(bf16[64,4,128]{2,0,1:T(8,128)(2,1)S(1)} %get-tuple-element.24), channel_id=1, source_target_pairs={{8,0},{16,8},{24,16},{32,24},{40,32},{48,40},{56,48},{64,56},{72,6... | collective-permute-start | bytes 196616 | tf_op jit(solution)/shard_map/ppermute | solution.py:18
  107.5 16.0 %copy-start.10 = (bf16[64,4,128]{2,0,1:T(8,128)(2,1)}, bf16[64,4,128]{2,0,1:T(8,128)(2,1)S(1)}, u32[]{:S(2)}) copy-start(bf16[64,4,128]{2,0,1:T(8,128)(2,1)S(1)} %collective-permute-done.12) | copy-start | bytes 196612
  117.0 6.9 %collective-permute-start.14 = (bf16[64,40,4]{0,1,2:T(8,128)(2,1)S(1)}, bf16[64,40,4]{0,1,2:T(8,128)(2,1)S(1)}, u32[]{:S(2)}, u32[]{:S(2)}) collective-permute-start(bf16[64,40,4]{0,1,2:T(8,128)(2,1)S(1)} %copy.21), channel_id=1, source_target_pairs={{0,1},{1,2},{2,3},{3,4},{4,5},{5,6},{6,7},{8,9},{9,10},{10,11},{11... | collective-permute-start | bytes 61448 | tf_op jit(solution)/shard_map/ppermute | solution.py:17
  119.4 5.4 %collective-permute-start.15 = (bf16[64,40,4]{0,1,2:T(8,128)(2,1)S(1)}, bf16[64,40,4]{0,1,2:T(8,128)(2,1)}, u32[]{:S(2)}, u32[]{:S(2)}) collective-permute-start(bf16[64,40,4]{0,1,2:T(8,128)(2,1)S(1)} %copy.23), channel_id=1, source_target_pairs={{1,0},{2,1},{3,2},{4,3},{5,4},{6,5},{7,6},{9,8},{10,9},{11,10},{12... | collective-permute-start | bytes 61448 | tf_op jit(solution)/shard_map/ppermute | solution.py:18
  125.9 2.2 %copy-start.7 = (bf16[64,576]{1,0:T(8,128)(2,1)S(1)}, bf16[64,576]{1,0:T(8,128)(2,1)}, u32[]{:S(2)}) copy-start(bf16[64,576]{1,0:T(8,128)(2,1)} %copy-done.6) | copy-start | bytes 221188
  132.2 6.0 %collective-permute-start.16 = (bf16[64,8,128]{2,0,1:T(8,128)(2,1)S(1)}, bf16[64,8,128]{2,0,1:T(8,128)(2,1)S(1)}, u32[]{:S(2)}, u32[]{:S(2)}) collective-permute-start(bf16[64,8,128]{2,0,1:T(8,128)(2,1)S(1)} %get-tuple-element.21), channel_id=1, source_target_pairs={{0,8},{8,16},{16,24},{24,32},{32,40},{40,48},{48,56},{56,64},{64,7... | collective-permute-start | bytes 393224 | tf_op jit(solution)/shard_map/ppermute | solution.py:17
  134.9 10.6 %collective-permute-start.17 = (bf16[64,8,128]{2,0,1:T(8,128)(2,1)S(1)}, bf16[64,8,128]{2,0,1:T(8,128)(2,1)S(1)}, u32[]{:S(2)}, u32[]{:S(2)}) collective-permute-start(bf16[64,8,128]{2,0,1:T(8,128)(2,1)S(1)} %get-tuple-element.22), channel_id=1, source_target_pairs={{8,0},{16,8},{24,16},{32,24},{40,32},{48,40},{56,48},{64,56},{72,6... | collective-permute-start | bytes 393224 | tf_op jit(solution)/shard_map/ppermute | solution.py:18
  148.3 11.8 %collective-permute-start.18 = (bf16[64,48,8]{0,2,1:T(8,128)(2,1)S(1)}, bf16[64,48,8]{0,2,1:T(8,128)(2,1)S(1)}, u32[]{:S(2)}, u32[]{:S(2)}) collective-permute-start(bf16[64,48,8]{0,2,1:T(8,128)(2,1)S(1)} %copy.25), channel_id=1, source_target_pairs={{0,1},{1,2},{2,3},{3,4},{4,5},{5,6},{6,7},{8,9},{9,10},{10,11},{11... | collective-permute-start | bytes 147464 | tf_op jit(solution)/shard_map/ppermute | solution.py:17
  153.7 6.9 %collective-permute-start.19 = (bf16[64,48,8]{0,2,1:T(8,128)(2,1)S(1)}, bf16[64,48,8]{0,2,1:T(8,128)(2,1)S(1)}, u32[]{:S(2)}, u32[]{:S(2)}) collective-permute-start(bf16[64,48,8]{0,2,1:T(8,128)(2,1)S(1)} %copy.27), channel_id=1, source_target_pairs={{1,0},{2,1},{3,2},{4,3},{5,4},{6,5},{7,6},{9,8},{10,9},{11,10},{12... | collective-permute-start | bytes 147464 | tf_op jit(solution)/shard_map/ppermute | solution.py:18
  161.7 2.7 %copy-start.5 = (bf16[64,576]{1,0:T(8,128)(2,1)S(1)}, bf16[64,576]{1,0:T(8,128)(2,1)}, u32[]{:S(2)}) copy-start(bf16[64,576]{1,0:T(8,128)(2,1)} %get-tuple-element.29) | copy-start | bytes 221188
  167.5 1.7 %copy-start.1 = (bf16[4352,256]{1,0:T(8,128)(2,1)S(1)}, bf16[4352,256]{1,0:T(8,128)(2,1)}, u32[]{:S(2)}) copy-start(bf16[4352,256]{1,0:T(8,128)(2,1)} %param.9) | copy-start | bytes 6684676
  (4 other events, 3.9 us)
where the time goes:
time: 171 us; the launch traced here: 169 us
  starting transfers between devices  65.8 us (38%)
  waiting for transfers between devices  53.3 us (31%)
  matrix products  22.5 us (13%)
  local copies, waits for them, and re-layouts  16.9 us (10%)
  other arithmetic  9.69 us (6%)
    ppermute x10, waiting for transfers between devices, padded_2(): after = lax.ppermute(leading, axis, down)  45.9 us
    ppermute x10, starting transfers between devices, padded_2(): before = lax.ppermute(last, axis, up)  35.7 us
    ppermute x10, starting transfers between devices, padded_2(): after = lax.ppermute(leading, axis, down)  24 us
    dot_general x36, matrix products, offset_sum(): jnp.einsum('oc,cij->oij', block, window_extent, preferred_element_type=jn...  20.1 us
    concatenate x8, other arithmetic, padded_2(): shard = jnp.concatenate([before, shard, after], axis=dim)  8.83 us
    all_to_all x1, waiting for transfers between devices, sent_to_all(): return lax.all_to_all(copies, axis, split_axis=0, concat_axis=0, tiled=True)  7.34 us
    all_to_all x1, starting transfers between devices, sent_to_all(): return lax.all_to_all(copies, axis, split_axis=0, concat_axis=0, tiled=True)  6.22 us
    ppermute x4, local copies, waits for them, and re-layouts, padded_2(): after = lax.ppermute(leading, axis, down)  4.59 us
  transfers between devices with their start and end apart: 21, of which 9 were waited for; matrix products, arithmetic and copies ran while one was open for 6% of the time, Pallas kernels for 0%

commit v1 on v0

v1 whole, which is shorter than its diff:
```python
import jax
import jax.numpy as jnp
from jax import lax
from jax.experimental import pallas as pl
from jax.experimental.pallas import tpu as pltpu
from jax.sharding import PartitionSpec as P

KERNEL = 17
HALF = KERNEL // 2
LAYERS = 4
WINDOW = 1024
VOCAB_PAD = 32
ROWS = 32
COLS = 128
HALO = 16
PLANES = ROWS + 2 * HALO
CH = 64
W = 256
f32, bf16 = jnp.float32, jnp.bfloat16


def elu(v):
    return jnp.maximum(v, jnp.exp(jnp.minimum(v, 0.0)) - 1.0)


def tables_kernel(table_ref, w_ref, out_ref):
    parts = [
        jnp.dot(table_ref[...], w_ref[pl.ds(k * W, W), :], preferred_element_type=f32)
        for k in range(KERNEL)
    ]
    out_ref[...] = jnp.concatenate(parts, axis=0).T.astype(bf16)


def pair_kernel(res_ref, tt_ref, w2_ref, pr_ref, pc_ref, pw_ref, out_ref, f_ref, x_ref, a_ref, b_ref, s_ref):
    row0 = lax.axis_index("row") * ROWS
    col0 = lax.axis_index("col") * COLS
    res = res_ref[...]
    span = res.shape[1]

    kinds = lax.broadcasted_iota(jnp.int32, (VOCAB_PAD, span), 0)
    hot = jnp.concatenate(
        [
            jnp.where(pltpu.roll(res, (span - k) % span, 1) == kinds, 1.0, 0.0).astype(bf16)
            for k in range(KERNEL)
        ],
        axis=0,
    )
    first_t = jnp.dot(tt_ref[...], hot, preferred_element_type=f32)
    lane = lax.broadcasted_iota(jnp.int32, (1, span), 1)
    pos = jnp.where(lane < 128, row0 - HALO - HALF + lane, col0 - HALO - HALF + lane - 128)
    first_t = jnp.where((pos >= 0) & (pos < WINDOW), elu(first_t), 0.0)
    f_ref[...] = first_t.T.astype(bf16).astype(f32)

    wide = COLS + 2 * HALO
    acc = jnp.zeros((PLANES + wide, W), f32)
    for k in range(KERNEL):
        lhs = jnp.concatenate([f_ref[pl.ds(k, PLANES), :], f_ref[pl.ds(128 + k, wide), :]], axis=0)
        acc = acc + jnp.dot(lhs.astype(bf16), w2_ref[pl.ds(k * W, W), :], preferred_element_type=f32)
    centre = jnp.concatenate([f_ref[pl.ds(HALF, PLANES), :], f_ref[pl.ds(128 + HALF, wide), :]], axis=0)
    second = (centre + elu(acc)).astype(bf16)

    nt = (((1,), (1,)), ((), ()))
    left = lax.dot_general(pr_ref[...], second[:PLANES], nt, preferred_element_type=f32)
    left = left.astype(bf16).astype(f32)
    starts = (PLANES, PLANES + 2 * HALO)
    right = jnp.concatenate(
        [
            lax.dot_general(pc_ref[...], second[s : s + COLS], nt, preferred_element_type=f32)
            for s in starts
        ],
        axis=1,
    )
    right = right.astype(bf16).astype(f32)

    lane2 = lax.broadcasted_iota(jnp.int32, (1, 2 * COLS), 1)
    col = col0 - HALO + lane2 - jnp.where(lane2 < COLS, 0, COLS - 2 * HALO)
    col_ok = jnp.where((col >= 0) & (col < WINDOW), 1.0, 0.0)

    def mask(plane):
        row = row0 - HALO + plane
        return jnp.where((row >= 0) & (row < WINDOW), col_ok, 0.0)

    def rows_of(plane):
        if isinstance(plane, int):
            return pl.ds(plane * CH, CH)
        return pl.ds(pl.multiple_of(plane * CH, CH), CH)

    for plane in range(1, PLANES - 1):
        x = (left[:, plane : plane + 1] + right).astype(bf16).astype(f32)
        x_ref[rows_of(plane), :] = x
        a_ref[rows_of(plane), :] = (elu(x) * mask(plane)).astype(bf16)

    def layer(number, low, high, src, dst, unroll):
        d = 2**number
        weights = pw_ref[number]

        def one(plane):
            stack = jnp.concatenate([src[rows_of(plane + (t - 1) * d), :] for t in range(3)], axis=0)
            y = jnp.dot(weights, stack, preferred_element_type=f32)
            tiles = []
            for t in range(2):
                part = y[:, t * COLS : (t + 1) * COLS]
                tiles.append(
                    pltpu.roll(part[:CH], d, 1) + part[CH : 2 * CH] + pltpu.roll(part[2 * CH :], COLS - d, 1)
                )
            if dst is None:
                a = tiles[0] + x_ref[rows_of(plane), :COLS]
                b = tiles[1] + x_ref[rows_of(plane), COLS:]
                a = pltpu.roll(a, COLS - HALO, 1)
                b = pltpu.roll(b, HALO, 1)
                lanes = lax.broadcasted_iota(jnp.int32, (1, COLS), 1)
                s_ref[pl.ds(plane - HALO, CH, stride=ROWS), :] = jnp.where(lanes < COLS // 2, a, b)
            else:
                x = x_ref[rows_of(plane), :] + jnp.concatenate(tiles, axis=1)
                x_ref[rows_of(plane), :] = x
                dst[rows_of(plane), :] = (elu(x) * mask(plane)).astype(bf16)

        def body(step, carry):
            for u in range(unroll):
                one(low + step * unroll + u)
            return carry

        lax.fori_loop(0, (high - low) // unroll, body, 0)

    layer(0, 2, 62, a_ref, b_ref, 4)
    layer(1, 4, 60, b_ref, a_ref, 4)
    layer(2, 8, 56, a_ref, b_ref, 4)
    layer(3, 16, 48, b_ref, None, 4)
    out_ref[...] = s_ref[...].reshape(CH, ROWS, COLS).astype(bf16)


def local(residues, embed_table, conv_first, conv_second, proj_row, proj_col, pair_weights):
    row, col = lax.axis_index("row"), lax.axis_index("col")
    copies = jnp.broadcast_to(residues, (lax.axis_size("row"), ROWS))
    every = lax.all_to_all(copies, "row", 0, 0, tiled=True).reshape(-1)
    every = jnp.pad(every, (ROWS, ROWS), constant_values=-1)
    rows_window = lax.dynamic_slice_in_dim(every, row * ROWS, 3 * ROWS)
    cols_window = lax.dynamic_slice_in_dim(every, col * COLS, COLS + 2 * ROWS)
    res = jnp.concatenate([rows_window, jnp.full((32,), -1, jnp.int32), cols_window, jnp.full((64,), -1, jnp.int32)])[None]

    table = jnp.pad(embed_table, ((0, VOCAB_PAD - embed_table.shape[0]), (0, 0)))
    tt = pl.pallas_call(
        tables_kernel,
        out_shape=jax.ShapeDtypeStruct((W, KERNEL * VOCAB_PAD), bf16),
        compiler_params=pltpu.CompilerParams(vmem_limit_bytes=16 * 2**20),
        cost_estimate=pl.CostEstimate(flops=2 * 32 * 4352 * 256, bytes_accessed=3 * 2**20, transcendentals=0),
    )(table, conv_first)
    pw = pair_weights.reshape(LAYERS, CH, 3, 3, CH).transpose(0, 3, 1, 2, 4).reshape(LAYERS, 3 * CH, 3 * CH)
    return pl.pallas_call(
        pair_kernel,
        out_shape=jax.ShapeDtypeStruct((CH, ROWS, COLS), bf16),
        scratch_shapes=[
            pltpu.VMEM((384, W), f32),
            pltpu.VMEM((PLANES * CH, 2 * COLS), f32),
            pltpu.VMEM((PLANES * CH, 2 * COLS), bf16),
            pltpu.VMEM((PLANES * CH, 2 * COLS), bf16),
            pltpu.VMEM((CH * ROWS, COLS), f32),
        ],
        compiler_params=pltpu.CompilerParams(vmem_limit_bytes=40 * 2**20),
        cost_estimate=pl.CostEstimate(flops=2 * 64 * 4096 * 2304, bytes_accessed=4 * 2**20, transcendentals=0),
    )(res, tt, conv_second, proj_row.T, proj_col.T, pw)


def solution(mesh):
    return jax.shard_map(
        local,
        mesh=mesh,
        in_specs=(P("row"), P(), P(), P(), P(), P(), P()),
        out_specs=P(None, "row", "col"),
        check_vma=False,
    )
```

time: 171 us -> 50.5 us (0.30)
  the two profiles are of different devices: /device:TPU:91 before, /device:TPU:1 now
where the time goes in v1:
time: 50.5 us; the launch traced here: 50.2 us
  Pallas kernels  24.2 us (48%)
  starting transfers between devices  12.8 us (25%)
  local copies, waits for them, and re-layouts  7.76 us (15%)
  waiting for transfers between devices  4.67 us (9%)
  other arithmetic  0.76 us (2%)
    pallas_call x1, Pallas kernels, local(): pl.pallas_call(pair_kernel, out_shape=jax.ShapeDtypeStruct((CH, ROWS, COL...  23.6 us
    all_to_all x1, starting transfers between devices, local(): every = lax.all_to_all(copies, 'row', 0, 0, tiled=True).reshape(-1)  12.8 us
    all_to_all x1, waiting for transfers between devices, local(): every = lax.all_to_all(copies, 'row', 0, 0, tiled=True).reshape(-1)  4.67 us
    unnamed x11, local copies, waits for them, and re-layouts  3.67 us
    transpose x1, local copies, waits for them, and re-layouts, local(): pair_weights.reshape(LAYERS, CH, 3, 3, CH).transpose(0, 3, 1, 2, 4)  1.48 us
    broadcast_in_dim x1, local copies, waits for them, and re-layouts, local(): copies = jnp.broadcast_to(residues, (lax.axis_size('row'), ROWS))  1.42 us
  transfers between devices with their start and end apart: 1, of which 1 were waited for; matrix products, arithmetic and copies ran while one was open for 8% of the time, Pallas kernels for 1%

profile of v1, /device:TPU:1, one launch (start us, length us, event | category | flops | bytes accessed | tf_op | source)
XLA Modules:
  0.0 50.2 jit_solution(7829211938362796150)
XLA Ops:
  0.0 0.0 copy-start.4
  0.0 0.0 copy-start
  0.0 1.4 %broadcast_in_dim.12 = s32[32,1,32]{2,1,0:T(1,128)} broadcast(s32[32]{0:T(128)} %param.7), dimensions={2} | broadcast | bytes 4224 | tf_op jit(solution)/shard_map/broadcast_in_dim | solution.py:134
  1.4 12.8 %all-to-all-start = ((s32[32,1,32]{2,1,0:T(1,128)}), s32[32,1,32]{2,1,0:T(1,128)S(1)}, u32[]{:S(2)}, u32[]{:S(2)}) async-start(s32[32,1,32]{2,1,0:T(1,128)} %broadcast_in_dim.12), calls=%async_computation | async-start | bytes 32768 | tf_op jit(solution)/shard_map/all_to_all | solution.py:135
  14.2 2.0 %copy.9 = bf16[4,64,576]{1,2,0:T(8,128)(2,1)} copy(bf16[4,64,576]{2,1,0:T(8,128)(2,1)} %param.13) | data formatting | bytes 589824 | tf_op args[6]
  16.2 1.5 %copy.10 = bf16[4,3,64,3,64]{4,3,2,1,0:T(4,128)(2,1)S(1)} copy(bf16[4,3,64,3,64]{2,4,1,3,0:T(8,128)(2,1)} %bitcast.7) | data formatting | bytes 589824 | tf_op jit(solution)/shard_map/transpose | solution.py:148
  17.7 0.0 copy-start.2
  17.7 0.0 copy-start.3
  17.7 0.4 reshape.16.pw_ref
  18.2 0.0 copy-done.4
  18.2 0.0 copy-done
  18.2 0.6 %shard_map.73.tt_ref = bf16[256,544]{1,0:T(8,128)(2,1)S(1)} custom-call(bf16[32,256]{1,0:T(8,128)(2,1)S(1)} %pad.9.table_ref, bf16[4352,256]{1,0:T(8,128)(2,1)S(1)} %copy-done), custom_call_target="tpu_custom_call" | custom-call | flops 71303168 | bytes 3145728 | tf_op jit(solution)/shard_map/pallas_call | solution.py:142
  18.8 4.7 %all-to-all-done = s32[32,1,32]{2,1,0:T(1,128)S(1)} async-done(((s32[32,1,32]{2,1,0:T(1,128)}), s32[32,1,32]{2,1,0:T(1,128)S(1)}, u32[]{:S(2)}, u32[]{:S(2)}) %all-to-all-start) | async-done | bytes 4128 | tf_op jit(solution)/shard_map/all_to_all | solution.py:135
  23.5 0.5 %broadcast.10 = s32[]{:T(128)} broadcast(s32[]{:T(128)} %constant.7.clone.1), dimensions={} | broadcast | bytes 8 | tf_op jit(solution)/shard_map/all_to_all | solution.py:135
  24.0 0.7 %reduce.3 = s32[32,32]{1,0:T(8,128)S(1)} reduce(s32[32,1,32]{2,1,0:T(1,128)S(1)} %all-to-all-done, s32[]{:T(128)} %broadcast.10), dimensions={1}, to_apply=%all_to_all.4.reduce_sub_computation.3 | reduce | bytes 8196 | tf_op jit(solution)/shard_map/all_to_all | solution.py:135
  24.7 0.1 reshape.14
  24.8 0.1 pad_dynamic-slice_fusion.1
  24.9 0.1 pad_dynamic-slice_fusion
  24.9 0.1 pad_add_fusion
  25.0 0.0 copy-done.2
  25.0 0.0 copy-done.3
  25.0 0.0 copy-start.1
  25.0 1.6 %copy-done.1 = bf16[4352,256]{1,0:T(8,128)(2,1)S(1)} copy-done((bf16[4352,256]{1,0:T(8,128)(2,1)S(1)}, bf16[4352,256]{1,0:T(8,128)(2,1)}, u32[]{:S(2)}) %copy-start.1) | copy-done | bytes 2228248
  26.7 23.6 %shard_map.74 = bf16[64,32,128]{2,1,0:T(8,128)(2,1)} custom-call(s32[1,384]{1,0:T(1,128)S(1)} %broadcast_in_dim.15.res_ref, bf16[256,544]{1,0:T(8,128)(2,1)S(1)} %shard_map.73.tt_ref, bf16[4352,256]{1,0:T(8,128)(2,1)S(1)} %copy-done.1, bf16[64,256]{1,0:T(8,128)(2,1)S(1)} %bitcast.5, bf16[64,256]{1,0:T(8,128)(2,1)S(1)} %bitcast.6, ...), custom_call_target="tpu_custom_call" | custom-call | flops 1207959552 | bytes 4194304 | tf_op jit(solution)/shard_map/pallas_call | solution.py:149
  (4 shorter events, 0.0 us)
Async XLA Ops:
  0.0 18.2 %copy-start.4 = (bf16[21,256]{1,0:T(8,128)(2,1)S(1)}, bf16[21,256]{1,0:T(8,128)(2,1)}, u32[]{:S(2)}) copy-start(bf16[21,256]{1,0:T(8,128)(2,1)} %param.8) | copy-start | bytes 32260
  0.0 18.2 %copy-start = (bf16[4352,256]{1,0:T(8,128)(2,1)S(1)}, bf16[4352,256]{1,0:T(8,128)(2,1)}, u32[]{:S(2)}) copy-start(bf16[4352,256]{1,0:T(8,128)(2,1)} %w_ref.1) | copy-start | bytes 6684676
  1.4 22.1 %all-to-all-start = ((s32[32,1,32]{2,1,0:T(1,128)}), s32[32,1,32]{2,1,0:T(1,128)S(1)}, u32[]{:S(2)}, u32[]{:S(2)}) async-start(s32[32,1,32]{2,1,0:T(1,128)} %broadcast_in_dim.12), calls=%async_computation | async-start | bytes 32768 | tf_op jit(solution)/shard_map/all_to_all | solution.py:135
  17.7 7.3 %copy-start.2 = (bf16[256,64]{0,1:T(8,128)(2,1)S(1)}, bf16[256,64]{0,1:T(8,128)(2,1)}, u32[]{:S(2)}) copy-start(bf16[256,64]{0,1:T(8,128)(2,1)} %param.11) | copy-start | bytes 98308
  17.7 7.3 %copy-start.3 = (bf16[256,64]{0,1:T(8,128)(2,1)S(1)}, bf16[256,64]{0,1:T(8,128)(2,1)}, u32[]{:S(2)}) copy-start(bf16[256,64]{0,1:T(8,128)(2,1)} %param.12) | copy-start | bytes 98308
  25.0 1.6 %copy-start.1 = (bf16[4352,256]{1,0:T(8,128)(2,1)S(1)}, bf16[4352,256]{1,0:T(8,128)(2,1)}, u32[]{:S(2)}) copy-start(bf16[4352,256]{1,0:T(8,128)(2,1)} %w2_ref.1) | copy-start | bytes 6684676

commit v2 on v1

v2 whole, which is shorter than its diff:
```python
import jax
import jax.numpy as jnp
from jax import lax
from jax.experimental import pallas as pl
from jax.experimental.pallas import tpu as pltpu
from jax.sharding import PartitionSpec as P

KERNEL = 17
HALF = KERNEL // 2
LAYERS = 4
WINDOW = 1024
VOCAB_PAD = 32
PIECES = (0, 5, 9, 13, 17)
ROWS = 32
COLS = 128
HALO = 16
PLANES = ROWS + 2 * HALO
CH = 64
W = 256
f32, bf16 = jnp.float32, jnp.bfloat16


def elu(v):
    return jnp.maximum(v, jnp.exp(jnp.minimum(v, 0.0)) - 1.0)


def tables_kernel(table_ref, w_hbm, out_ref, w_ref, sems):
    copies = [
        pltpu.make_async_copy(w_hbm.at[pl.ds(a * W, (b - a) * W)], w_ref.at[pl.ds(a * W, (b - a) * W)], sems.at[n])
        for n, (a, b) in enumerate(zip(PIECES, PIECES[1:]))
    ]
    for copy in copies:
        copy.start()
    parts = []
    for k in range(KERNEL):
        if k in PIECES:
            copies[PIECES.index(k)].wait()
        parts.append(jnp.dot(table_ref[...], w_ref[pl.ds(k * W, W), :], preferred_element_type=f32))
    out_ref[...] = jnp.concatenate(parts, axis=0).T.astype(bf16)


def pair_kernel(res_ref, tt_ref, w2_ref, pr_ref, pc_ref, pw_ref, out_ref, f_ref, x_ref, a_ref, b_ref, s_ref):
    row, column = lax.axis_index("row"), lax.axis_index("col")
    row0, col0 = row * ROWS, column * COLS
    blocks = res_ref.shape[0]
    span = 384

    def block(number):
        return res_ref[jnp.clip(number, 0, blocks - 1)]

    rows_blocks = [block(row - 1 + t) for t in range(3)]
    cols_blocks = [block(column * (COLS // ROWS) - 1 + t) for t in range(6)]
    res = jnp.concatenate(rows_blocks + rows_blocks[:1] + cols_blocks + cols_blocks[:2], axis=1)
    lane = lax.broadcasted_iota(jnp.int32, (1, span), 1)
    pos = jnp.where(lane < 128, row0 + lane, col0 + lane - 128)
    res = jnp.where((pos >= ROWS) & (pos < WINDOW + ROWS), res, -1)

    kinds = lax.broadcasted_iota(jnp.int32, (VOCAB_PAD, span), 0)
    hot = jnp.concatenate(
        [
            jnp.where(pltpu.roll(res, (span - k) % span, 1) == kinds, 1.0, 0.0).astype(bf16)
            for k in range(KERNEL)
        ],
        axis=0,
    )
    first_t = jnp.dot(tt_ref[...], hot, preferred_element_type=f32)
    pos = pos - HALO - HALF
    first_t = jnp.where((pos >= 0) & (pos < WINDOW), elu(first_t), 0.0)
    f_ref[...] = first_t.T.astype(bf16).astype(f32)

    wide = COLS + 2 * HALO
    acc = jnp.zeros((PLANES + wide, W), f32)
    for k in range(KERNEL):
        lhs = jnp.concatenate([f_ref[pl.ds(k, PLANES), :], f_ref[pl.ds(128 + k, wide), :]], axis=0)
        acc = acc + jnp.dot(lhs.astype(bf16), w2_ref[pl.ds(k * W, W), :], preferred_element_type=f32)
    centre = jnp.concatenate([f_ref[pl.ds(HALF, PLANES), :], f_ref[pl.ds(128 + HALF, wide), :]], axis=0)
    second = (centre + elu(acc)).astype(bf16)

    nt = (((1,), (1,)), ((), ()))
    left = lax.dot_general(pr_ref[...], second[:PLANES], nt, preferred_element_type=f32)
    left = left.astype(bf16).astype(f32)
    cols_t = second[PLANES:]
    order_a = jnp.concatenate([cols_t[HALO:COLS], cols_t[:HALO]], axis=0)
    order_b = jnp.concatenate([cols_t[COLS + HALO :], cols_t[2 * HALO : COLS + HALO]], axis=0)
    right = jnp.concatenate(
        [lax.dot_general(pc_ref[...], o, nt, preferred_element_type=f32) for o in (order_a, order_b)],
        axis=1,
    )
    right = right.astype(bf16).astype(f32)

    lane2 = lax.broadcasted_iota(jnp.int32, (CH, 2 * COLS), 1)
    tile_col = jnp.where(
        lane2 < COLS,
        jnp.where(lane2 < COLS - HALO, lane2, lane2 - COLS),
        jnp.where(lane2 < COLS + HALO, lane2, lane2 - COLS),
    )
    col = col0 + tile_col
    col_ok = jnp.where((col >= 0) & (col < WINDOW), 1.0, 0.0).astype(bf16)

    def activate(x, plane):
        ok = col_ok
        if plane < HALO or plane >= PLANES - HALO:
            at = row0 - HALO + plane
            ok = col_ok * jnp.where((at >= 0) & (at < WINDOW), 1.0, 0.0).astype(bf16)
        return elu(x) * ok

    def rows_of(plane):
        return pl.ds(plane * CH, CH)

    for plane in range(1, PLANES - 1):
        x = (left[:, plane : plane + 1] + right).astype(bf16)
        x_ref[rows_of(plane), :] = x
        a_ref[rows_of(plane), :] = activate(x, plane)

    def layer(number, low, high, src, dst):
        d = 2**number
        weights = pw_ref[number]
        lanes = lax.broadcasted_iota(jnp.int32, (CH, COLS), 1)
        for plane in range(low, high):
            stack = [src[rows_of(plane + (t - 1) * d), :] for t in range(3)] + [x_ref[rows_of(plane), :]]
            y = jnp.dot(weights, jnp.concatenate(stack, axis=0), preferred_element_type=f32)
            before, here, after = y[:CH], y[CH : 2 * CH], y[2 * CH :]
            if dst is None:
                half = COLS // 2
                before = jnp.where((lanes < half - d) | (lanes >= COLS - d), before[:, :COLS], before[:, COLS:])
                here = jnp.where(lanes < half, here[:, :COLS], here[:, COLS:])
                after = jnp.where((lanes >= d) & (lanes < half + d), after[:, :COLS], after[:, COLS:])
                total = pltpu.roll(before, d, 1) + here + pltpu.roll(after, COLS - d, 1)
                s_ref[pl.ds(plane - HALO, CH, stride=ROWS), :] = total
            else:
                x = jnp.concatenate(
                    [
                        pltpu.roll(before[:, s], d, 1) + here[:, s] + pltpu.roll(after[:, s], COLS - d, 1)
                        for s in (slice(0, COLS), slice(COLS, 2 * COLS))
                    ],
                    axis=1,
                ).astype(bf16)
                x_ref[rows_of(plane), :] = x
                dst[rows_of(plane), :] = activate(x, plane)

    layer(0, 2, 62, a_ref, b_ref)
    layer(1, 4, 60, b_ref, a_ref)
    layer(2, 8, 56, a_ref, b_ref)
    layer(3, 16, 48, b_ref, None)
    out_ref[...] = s_ref[...].reshape(CH, ROWS, COLS).astype(bf16)


def local(residues, embed_table, conv_first, conv_second, proj_row, proj_col, pair_weights):
    vmem = pl.BlockSpec(memory_space=pltpu.VMEM)
    copies = jnp.broadcast_to(residues, (lax.axis_size("row"), 1, ROWS))
    every = lax.all_to_all(copies, "row", 0, 0, tiled=True)
    table = jnp.pad(embed_table, ((0, VOCAB_PAD - embed_table.shape[0]), (0, 0)))
    tt = pl.pallas_call(
        tables_kernel,
        in_specs=[vmem, pl.BlockSpec(memory_space=pl.ANY)],
        out_specs=vmem,
        out_shape=jax.ShapeDtypeStruct((W, KERNEL * VOCAB_PAD), bf16),
        scratch_shapes=[pltpu.VMEM((KERNEL * W, W), bf16), pltpu.SemaphoreType.DMA((len(PIECES) - 1,))],
        compiler_params=pltpu.CompilerParams(vmem_limit_bytes=60 * 2**20),
        cost_estimate=pl.CostEstimate(flops=2 * 32 * 4352 * 256, bytes_accessed=3 * 2**20, transcendentals=0),
    )(table, conv_first)
    pw = pair_weights.reshape(LAYERS, CH, 3, 3, CH).transpose(0, 3, 1, 2, 4).reshape(LAYERS, 3 * CH, 3 * CH)
    same = jnp.eye(3 * CH, CH, k=-CH, dtype=bf16)
    pw = jnp.concatenate([pw, jnp.broadcast_to(same, (LAYERS, *same.shape))], axis=2)
    return pl.pallas_call(
        pair_kernel,
        out_shape=jax.ShapeDtypeStruct((CH, ROWS, COLS), bf16),
        scratch_shapes=[
            pltpu.VMEM((384, W), f32),
            pltpu.VMEM((PLANES * CH, 2 * COLS), bf16),
            pltpu.VMEM((PLANES * CH, 2 * COLS), bf16),
            pltpu.VMEM((PLANES * CH, 2 * COLS), bf16),
            pltpu.VMEM((CH * ROWS, COLS), f32),
        ],
        compiler_params=pltpu.CompilerParams(vmem_limit_bytes=24 * 2**20),
        cost_estimate=pl.CostEstimate(flops=2 * 64 * 4096 * 2304, bytes_accessed=4 * 2**20, transcendentals=0),
    )(every, tt, conv_second, proj_row.T, proj_col.T, pw)


def solution(mesh):
    return jax.shard_map(
        local,
        mesh=mesh,
        in_specs=(P("row"), P(), P(), P(), P(), P(), P()),
        out_specs=P(None, "row", "col"),
        check_vma=False,
    )
```

time: 50.5 us -> 35.2 us (0.70)
  Pallas kernels: 24.2 us -> 14.1 us
  local copies, waits for them, and re-layouts: 7.76 us -> 5.18 us
  waiting for transfers between devices: 4.67 us -> 2.58 us
  other arithmetic: 0.76 us -> 0.25 us
    pallas_call x1, Pallas kernels: 23.6 us -> 10.6 us  [local(): pl.pallas_call(pair_kernel, out_shape=jax.ShapeDtypeStruct((CH, ROWS, COL...]
    pallas_call x1, Pallas kernels: 0.6 us -> 3.52 us  [local(): pl.pallas_call(tables_kernel, in_specs=[vmem, pl.BlockSpec(memory_space=p...]
    all_to_all x1, waiting for transfers between devices: 4.67 us -> 2.58 us  [local(): every = lax.all_to_all(copies, 'row', 0, 0, tiled=True)]
    unnamed x11, local copies, waits for them, and re-layouts: 3.67 us -> 2.26 us
    transpose x1, local copies, waits for them, and re-layouts: 1.48 us -> 0.58 us  [local(): pair_weights.reshape(LAYERS, CH, 3, 3, CH).transpose(0, 3, 1, 2, 4)]
    all_to_all x1 -> x0, other arithmetic: 0.69 us -> none  [local(): every = lax.all_to_all(copies, 'row', 0, 0, tiled=True).reshape(-1)]
    pad x1, local copies, waits for them, and re-layouts: 0.01 us -> 0.6 us  [local(): jnp.pad(embed_table, ((0, VOCAB_PAD - embed_table.shape[0]), (0, 0)))]
    all_to_all x1 -> x0, local copies, waits for them, and re-layouts: 0.51 us -> none  [local(): every = lax.all_to_all(copies, 'row', 0, 0, tiled=True).reshape(-1)]
  transfers between devices with their start and end apart: 1 -> 1, of which waited for: 1 -> 1; matrix products, arithmetic and copies ran while one was open for 8% -> 9% of each run, Pallas kernels for 1% -> 10%
where the time goes in v2:
time: 35.2 us; the launch traced here: 35 us
  Pallas kernels  14.1 us (40%)
  starting transfers between devices  12.8 us (36%)
  local copies, waits for them, and re-layouts  5.18 us (15%)
  waiting for transfers between devices  2.58 us (7%)
    all_to_all x1, starting transfers between devices, local(): every = lax.all_to_all(copies, 'row', 0, 0, tiled=True)  12.8 us
    pallas_call x1, Pallas kernels, local(): pl.pallas_call(pair_kernel, out_shape=jax.ShapeDtypeStruct((CH, ROWS, COL...  10.6 us
    pallas_call x1, Pallas kernels, local(): pl.pallas_call(tables_kernel, in_specs=[vmem, pl.BlockSpec(memory_space=p...  3.52 us
    all_to_all x1, waiting for transfers between devices, local(): every = lax.all_to_all(copies, 'row', 0, 0, tiled=True)  2.58 us
    unnamed x11, local copies, waits for them, and re-layouts  2.26 us
    broadcast_in_dim x1, local copies, waits for them, and re-layouts, local(): copies = jnp.broadcast_to(residues, (lax.axis_size('row'), 1, ROWS))  1.26 us
  transfers between devices with their start and end apart: 1, of which 1 were waited for; matrix products, arithmetic and copies ran while one was open for 9% of the time, Pallas kernels for 10%

profile of v2, /device:TPU:1, one launch (start us, length us, event | category | flops | bytes accessed | tf_op | source)
XLA Modules:
  0.0 35.0 jit_solution(8421996744296478432)
XLA Ops:
  0.0 1.3 %broadcast_in_dim.6 = s32[32,1,32]{2,1,0:T(1,128)} broadcast(s32[32]{0:T(128)} %param.7), dimensions={2} | broadcast | bytes 4224 | tf_op jit(solution)/shard_map/broadcast_in_dim | solution.py:150
  1.3 12.8 %all-to-all-start = ((s32[32,1,32]{2,1,0:T(1,128)}), s32[32,1,32]{2,1,0:T(1,128)S(1)}, u32[]{:S(2)}, u32[]{:S(2)}) async-start(s32[32,1,32]{2,1,0:T(1,128)} %broadcast_in_dim.6), calls=%async_computation | async-start | bytes 32768 | tf_op jit(solution)/shard_map/all_to_all | solution.py:151
  14.0 0.0 copy-start.4
  14.1 1.3 %copy.9 = bf16[4,64,576]{1,2,0:T(8,128)(2,1)S(1)} copy(bf16[4,64,576]{2,1,0:T(8,128)(2,1)} %param.13) | data formatting | bytes 589824 | tf_op args[6]
  15.3 0.6 %copy.10 = bf16[4,3,64,3,64]{4,3,2,1,0:T(4,128)(2,1)S(1)} copy(bf16[4,3,64,3,64]{2,4,1,3,0:T(8,128)(2,1)S(1)} %bitcast.7) | data formatting | bytes 589824 | tf_op jit(solution)/shard_map/transpose | solution.py:162
  15.9 0.4 %reshape.7 = bf16[4,192,192]{2,1,0:T(8,128)(2,1)S(1)} reshape(bf16[4,3,64,3,64]{4,3,2,1,0:T(4,128)(2,1)S(1)} %copy.10) | data formatting | bytes 589824 | tf_op jit(solution)/shard_map/reshape | solution.py:162
  16.4 0.0 copy-start.1
  16.4 0.0 copy-start.2
  16.4 0.0 copy-start.3
  16.4 0.1 fusion
  16.5 0.2 pad_maximum_fusion.pw_ref
  16.7 0.0 copy-done.4
  16.7 0.6 %pad.4.table_ref = bf16[32,256]{1,0:T(8,128)(2,1)} pad(bf16[21,256]{1,0:T(8,128)(2,1)S(1)} %copy-done.4, bf16[]{:T(256)} %constant.1.clone.1), padding=0_11x0_0 | pad | bytes 27138 | tf_op jit(solution)/shard_map/jit(_pad)/pad | solution.py:152
  17.3 3.5 %shard_map.73.tt_ref = bf16[256,544]{1,0:T(8,128)(2,1)} custom-call(bf16[32,256]{1,0:T(8,128)(2,1)} %pad.4.table_ref, bf16[4352,256]{1,0:T(8,128)(2,1)} %w_hbm.1), custom_call_target="tpu_custom_call" | custom-call | flops 71303168 | bytes 3145728 | tf_op jit(solution)/shard_map/pallas_call | solution.py:153
  20.8 2.6 %all-to-all-done.res_ref = s32[32,1,32]{2,1,0:T(1,128)S(1)} async-done(((s32[32,1,32]{2,1,0:T(1,128)}), s32[32,1,32]{2,1,0:T(1,128)S(1)}, u32[]{:S(2)}, u32[]{:S(2)}) %all-to-all-start) | async-done | bytes 4128 | tf_op jit(solution)/shard_map/all_to_all | solution.py:151
  23.4 0.0 copy-done.1
  23.4 0.0 copy-done.2
  23.4 0.0 copy-done.3
  23.4 0.0 copy-start
  23.4 1.0 %copy-done = bf16[256,544]{1,0:T(8,128)(2,1)S(1)} copy-done((bf16[256,544]{1,0:T(8,128)(2,1)S(1)}, bf16[256,544]{1,0:T(8,128)(2,1)}, u32[]{:S(2)}) %copy-start) | copy-done | bytes 278552
  24.4 10.6 %shard_map.74 = bf16[64,32,128]{2,1,0:T(8,128)(2,1)} custom-call(s32[32,1,32]{2,1,0:T(1,128)S(1)} %all-to-all-done.res_ref, bf16[256,544]{1,0:T(8,128)(2,1)S(1)} %copy-done, bf16[4352,256]{1,0:T(8,128)(2,1)S(1)} %copy-done.1, bf16[64,256]{1,0:T(8,128)(2,1)S(1)} %bitcast.5, bf16[64,256]{1,0:T(8,128)(2,1)S(1)} %bitcast.6, ...), custom_call_target="tpu_custom_call" | custom-call | flops 1207959552 | bytes 4194304 | tf_op jit(solution)/shard_map/pallas_call | solution.py:165
  (2 shorter events, 0.0 us)
Async XLA Ops:
  1.3 22.1 %all-to-all-start = ((s32[32,1,32]{2,1,0:T(1,128)}), s32[32,1,32]{2,1,0:T(1,128)S(1)}, u32[]{:S(2)}, u32[]{:S(2)}) async-start(s32[32,1,32]{2,1,0:T(1,128)} %broadcast_in_dim.6), calls=%async_computation | async-start | bytes 32768 | tf_op jit(solution)/shard_map/all_to_all | solution.py:151
  14.0 2.6 %copy-start.4 = (bf16[21,256]{1,0:T(8,128)(2,1)S(1)}, bf16[21,256]{1,0:T(8,128)(2,1)}, u32[]{:S(2)}) copy-start(bf16[21,256]{1,0:T(8,128)(2,1)} %param.8) | copy-start | bytes 32260
  16.4 7.1 %copy-start.1 = (bf16[4352,256]{1,0:T(8,128)(2,1)S(1)}, bf16[4352,256]{1,0:T(8,128)(2,1)}, u32[]{:S(2)}) copy-start(bf16[4352,256]{1,0:T(8,128)(2,1)} %w2_ref.1) | copy-start | bytes 6684676
  16.4 7.0 %copy-start.2 = (bf16[256,64]{0,1:T(8,128)(2,1)S(1)}, bf16[256,64]{0,1:T(8,128)(2,1)}, u32[]{:S(2)}) copy-start(bf16[256,64]{0,1:T(8,128)(2,1)} %param.11) | copy-start | bytes 98308
  16.4 7.0 %copy-start.3 = (bf16[256,64]{0,1:T(8,128)(2,1)S(1)}, bf16[256,64]{0,1:T(8,128)(2,1)}, u32[]{:S(2)}) copy-start(bf16[256,64]{0,1:T(8,128)(2,1)} %param.12) | copy-start | bytes 98308
  23.4 1.0 %copy-start = (bf16[256,544]{1,0:T(8,128)(2,1)S(1)}, bf16[256,544]{1,0:T(8,128)(2,1)}, u32[]{:S(2)}) copy-start(bf16[256,544]{1,0:T(8,128)(2,1)} %shard_map.73.tt_ref) | copy-start | bytes 835588

commit v3 on v2

--- a/solution.py
+++ b/solution.py
@@ -16,6 +16,7 @@
 HALO = 16
 PLANES = ROWS + 2 * HALO
 CH = 64
+BLOCK = 16
 W = 256
 f32, bf16 = jnp.float32, jnp.bfloat16
 
@@ -88,7 +89,7 @@
     )
     right = right.astype(bf16).astype(f32)
 
-    lane2 = lax.broadcasted_iota(jnp.int32, (CH, 2 * COLS), 1)
+    lane2 = lax.broadcasted_iota(jnp.int32, (BLOCK, 2 * COLS), 1)
     tile_col = jnp.where(
         lane2 < COLS,
         jnp.where(lane2 < COLS - HALO, lane2, lane2 - COLS),
@@ -108,35 +109,38 @@
         return pl.ds(plane * CH, CH)
 
     for plane in range(1, PLANES - 1):
-        x = (left[:, plane : plane + 1] + right).astype(bf16)
-        x_ref[rows_of(plane), :] = x
-        a_ref[rows_of(plane), :] = activate(x, plane)
+        for first in range(0, CH, BLOCK):
+            block_of = slice(first, first + BLOCK)
+            x = (left[block_of, plane : plane + 1] + right[block_of]).astype(bf16)
+            x_ref[pl.ds(plane * CH + first, BLOCK), :] = x
+            a_ref[pl.ds(plane * CH + first, BLOCK), :] = activate(x, plane)
 
     def layer(number, low, high, src, dst):
         d = 2**number
         weights = pw_ref[number]
-        lanes = lax.broadcasted_iota(jnp.int32, (CH, COLS), 1)
+        lanes = lax.broadcasted_iota(jnp.int32, (BLOCK, COLS), 1)
         for plane in range(low, high):
             stack = [src[rows_of(plane + (t - 1) * d), :] for t in range(3)] + [x_ref[rows_of(plane), :]]
             y = jnp.dot(weights, jnp.concatenate(stack, axis=0), preferred_element_type=f32)
-            before, here, after = y[:CH], y[CH : 2 * CH], y[2 * CH :]
-            if dst is None:
-                half = COLS // 2
-                before = jnp.where((lanes < half - d) | (lanes >= COLS - d), before[:, :COLS], before[:, COLS:])
-                here = jnp.where(lanes < half, here[:, :COLS], here[:, COLS:])
-                after = jnp.where((lanes >= d) & (lanes < half + d), after[:, :COLS], after[:, COLS:])
-                total = pltpu.roll(before, d, 1) + here + pltpu.roll(after, COLS - d, 1)
-                s_ref[pl.ds(plane - HALO, CH, stride=ROWS), :] = total
-            else:
-                x = jnp.concatenate(
-                    [
-                        pltpu.roll(before[:, s], d, 1) + here[:, s] + pltpu.roll(after[:, s], COLS - d, 1)
-                        for s in (slice(0, COLS), slice(COLS, 2 * COLS))
-                    ],
-                    axis=1,
-                ).astype(bf16)
-                x_ref[rows_of(plane), :] = x
-                dst[rows_of(plane), :] = activate(x, plane)
+            for first in range(0, CH, BLOCK):
+                before, here, after = (y[3 * first + t * BLOCK : 3 * first + (t + 1) * BLOCK] for t in range(3))
+                if dst is None:
+                    half = COLS // 2
+                    before = jnp.where((lanes < half - d) | (lanes >= COLS - d), before[:, :COLS], before[:, COLS:])
+                    here = jnp.where(lanes < half, here[:, :COLS], here[:, COLS:])
+                    after = jnp.where((lanes >= d) & (lanes < half + d), after[:, :COLS], after[:, COLS:])
+                    total = pltpu.roll(before, d, 1) + here + pltpu.roll(after, COLS - d, 1)
+                    s_ref[pl.ds(first * ROWS + plane - HALO, BLOCK, stride=ROWS), :] = total
+                else:
+                    x = jnp.concatenate(
+                        [
+                            pltpu.roll(before[:, s], d, 1) + here[:, s] + pltpu.roll(after[:, s], COLS - d, 1)
+                            for s in (slice(0, COLS), slice(COLS, 2 * COLS))
+                        ],
+                        axis=1,
+                    ).astype(bf16)
+                    x_ref[pl.ds(plane * CH + first, BLOCK), :] = x
+                    dst[pl.ds(plane * CH + first, BLOCK), :] = activate(x, plane)
 
     layer(0, 2, 62, a_ref, b_ref)
     layer(1, 4, 60, b_ref, a_ref)
@@ -156,11 +160,15 @@
         out_specs=vmem,
         out_shape=jax.ShapeDtypeStruct((W, KERNEL * VOCAB_PAD), bf16),
         scratch_shapes=[pltpu.VMEM((KERNEL * W, W), bf16), pltpu.SemaphoreType.DMA((len(PIECES) - 1,))],
-        compiler_params=pltpu.CompilerParams(vmem_limit_bytes=60 * 2**20),
+        compiler_params=pltpu.CompilerParams(vmem_limit_bytes=40 * 2**20),
         cost_estimate=pl.CostEstimate(flops=2 * 32 * 4352 * 256, bytes_accessed=3 * 2**20, transcendentals=0),
     )(table, conv_first)
-    pw = pair_weights.reshape(LAYERS, CH, 3, 3, CH).transpose(0, 3, 1, 2, 4).reshape(LAYERS, 3 * CH, 3 * CH)
-    same = jnp.eye(3 * CH, CH, k=-CH, dtype=bf16)
+    tt, pair_weights = lax.optimization_barrier((tt, pair_weights))
+    blocks = CH // BLOCK
+    pw = pair_weights.reshape(LAYERS, blocks, BLOCK, 3, 3, CH).transpose(0, 1, 4, 2, 3, 5)
+    pw = pw.reshape(LAYERS, 3 * CH, 3 * CH)
+    same = jnp.eye(3 * CH, CH, k=-CH, dtype=bf16).reshape(3, blocks, BLOCK, CH)
+    same = same.transpose(1, 0, 2, 3).reshape(3 * CH, CH)
     pw = jnp.concatenate([pw, jnp.broadcast_to(same, (LAYERS, *same.shape))], axis=2)
     return pl.pallas_call(
         pair_kernel,

time: 35.2 us -> 34.1 us (0.969)
  local copies, waits for them, and re-layouts: 5.18 us -> 7.99 us
  waiting for transfers between devices: 2.58 us -> 0.06 us
  Pallas kernels: 14.1 us -> 11.7 us
  other arithmetic: 0.25 us -> 1.25 us
    all_to_all x1, waiting for transfers between devices: 2.58 us -> 0.06 us  [local(): every = lax.all_to_all(copies, 'row', 0, 0, tiled=True)]
    pallas_call x1, Pallas kernels: 3.52 us -> 1.3 us  [local(): pl.pallas_call(tables_kernel, in_specs=[vmem, pl.BlockSpec(memory_space=p...]
    reshape x1 -> x2, local copies, waits for them, and re-layouts: 0.44 us -> 2.53 us  [the longest x1 1.34 us: local(): pair_weights.reshape(LAYERS, blocks, BLOCK, 3, 3, CH)]
    transpose x1, local copies, waits for them, and re-layouts: 0.58 us -> 1.73 us  [local(): pair_weights.reshape(LAYERS, blocks, BLOCK, 3, 3, CH)]
    concatenate x1, other arithmetic: 0.16 us -> 1.15 us  [local(): jnp.concatenate([pw, jnp.broadcast_to(same, (LAYERS, *same.shape))], axis=2)]
    unnamed x11 -> x10, local copies, waits for them, and re-layouts: 2.26 us -> 1.64 us
  transfers between devices with their start and end apart: 1 -> 1, of which waited for: 1 -> 1; matrix products, arithmetic and copies ran while one was open for 9% -> 19% of each run, Pallas kernels for 10% -> 4%
where the time goes in v3:
time: 34.1 us; the launch traced here: 33.8 us
  starting transfers between devices  12.8 us (38%)
  Pallas kernels  11.7 us (34%)
  local copies, waits for them, and re-layouts  7.99 us (23%)
  other arithmetic  1.25 us (4%)
    all_to_all x1, starting transfers between devices, local(): every = lax.all_to_all(copies, 'row', 0, 0, tiled=True)  12.8 us
    pallas_call x1, Pallas kernels, local(): pl.pallas_call(pair_kernel, out_shape=jax.ShapeDtypeStruct((CH, ROWS, COL...  10.4 us
    transpose x1, local copies, waits for them, and re-layouts, local(): pair_weights.reshape(LAYERS, blocks, BLOCK, 3, 3, CH)  1.73 us
    unnamed x10, local copies, waits for them, and re-layouts  1.64 us
    reshape x1, local copies, waits for them, and re-layouts, local(): pair_weights.reshape(LAYERS, blocks, BLOCK, 3, 3, CH)  1.34 us
    pallas_call x1, Pallas kernels, local(): pl.pallas_call(tables_kernel, in_specs=[vmem, pl.BlockSpec(memory_space=p...  1.3 us
    broadcast_in_dim x1, local copies, waits for them, and re-layouts, local(): copies = jnp.broadcast_to(residues, (lax.axis_size('row'), 1, ROWS))  1.26 us
    reshape x1, local copies, waits for them, and re-layouts, local(): pw = pw.reshape(LAYERS, 3 * CH, 3 * CH)  1.19 us
  transfers between devices with their start and end apart: 1, of which 1 were waited for; matrix products, arithmetic and copies ran while one was open for 19% of the time, Pallas kernels for 4%

profile of v3, /device:TPU:1, one launch (start us, length us, event | category | flops | bytes accessed | tf_op | source)
XLA Modules:
  0.0 33.8 jit_solution(13889951825766088659)
XLA Ops:
  0.0 1.3 %broadcast_in_dim.6 = s32[32,1,32]{2,1,0:T(1,128)} broadcast(s32[32]{0:T(128)} %param.7), dimensions={2} | broadcast | bytes 4224 | tf_op jit(solution)/shard_map/broadcast_in_dim | solution.py:154
  1.3 12.8 %all-to-all-start = ((s32[32,1,32]{2,1,0:T(1,128)}), s32[32,1,32]{2,1,0:T(1,128)S(1)}, u32[]{:S(2)}, u32[]{:S(2)}) async-start(s32[32,1,32]{2,1,0:T(1,128)} %broadcast_in_dim.6), calls=%async_computation | async-start | bytes 32768 | tf_op jit(solution)/shard_map/all_to_all | solution.py:155
  14.0 0.7 %pad.4.table_ref = bf16[32,256]{1,0:T(8,128)(2,1)S(1)} pad(bf16[21,256]{1,0:T(8,128)(2,1)} %param.8, bf16[]{:T(256)} %constant.5.clone.1), padding=0_11x0_0 | pad | bytes 27138 | tf_op jit(solution)/shard_map/jit(_pad)/pad | solution.py:156
  14.8 0.0 copy-start
  14.8 1.6 %copy-done = bf16[4352,256]{1,0:T(8,128)(2,1)S(1)} copy-done((bf16[4352,256]{1,0:T(8,128)(2,1)S(1)}, bf16[4352,256]{1,0:T(8,128)(2,1)}, u32[]{:S(2)}) %copy-start) | copy-done | bytes 2228248
  16.4 0.0 copy-start.4
  16.4 1.3 %shard_map.73.tt_ref = bf16[256,544]{1,0:T(8,128)(2,1)S(1)} custom-call(bf16[32,256]{1,0:T(8,128)(2,1)S(1)} %pad.4.table_ref, bf16[4352,256]{1,0:T(8,128)(2,1)S(1)} %copy-done), custom_call_target="tpu_custom_call" | custom-call | flops 71303168 | bytes 3145728 | tf_op jit(solution)/shard_map/pallas_call | solution.py:157
  17.7 0.0 copy-done.4
  17.7 1.3 %reshape.27 = bf16[4,4,16,3,3,64]{5,4,3,2,1,0:T(4,128)(2,1)} reshape(bf16[4,64,576]{2,1,0:T(8,128)(2,1)S(1)} %copy-done.4) | data formatting | bytes 589824 | tf_op jit(solution)/shard_map/reshape | solution.py:168
  19.0 0.0 copy-start.1
  19.0 0.0 copy-start.2
  19.1 0.0 copy-start.3
  19.1 1.7 %copy.9 = bf16[4,4,3,16,3,64]{5,4,3,2,1,0:T(4,128)(2,1)S(1)} copy(bf16[4,4,3,16,3,64]{5,2,4,3,1,0:T(4,128)(2,1)} %bitcast.5) | data formatting | bytes 589824 | tf_op jit(solution)/shard_map/transpose | solution.py:168
  20.8 1.2 %reshape.28 = bf16[4,192,192]{2,1,0:T(8,128)(2,1)} reshape(bf16[4,4,3,16,3,64]{5,4,3,2,1,0:T(4,128)(2,1)S(1)} %copy.9) | data formatting | bytes 589824 | tf_op jit(solution)/shard_map/reshape | solution.py:169
  22.0 0.1 add.25
  22.1 0.1 fusion
  22.2 1.1 %pad_maximum_fusion.pw_ref = bf16[4,192,256]{2,1,0:T(8,128)(2,1)S(1)} fusion(bf16[4,192,64]{2,1,0:T(8,128)(2,1)S(1)} %broadcast_in_dim.7, bf16[4,192,192]{2,1,0:T(8,128)(2,1)} %reshape.28), kind=kLoop, calls=%fused_computation | loop fusion | flops 786432 | bytes 786432 | tf_op jit(solution)/shard_map/concatenate | solution.py:172
  23.3 0.1 all-to-all-done.res_ref
  23.4 0.0 copy-done.1
  23.4 0.0 copy-done.2
  23.4 0.0 copy-done.3
  23.4 10.4 %shard_map.74 = bf16[64,32,128]{2,1,0:T(8,128)(2,1)} custom-call(s32[32,1,32]{2,1,0:T(1,128)S(1)} %all-to-all-done.res_ref, bf16[256,544]{1,0:T(8,128)(2,1)S(1)} %shard_map.73.tt_ref, bf16[4352,256]{1,0:T(8,128)(2,1)S(1)} %copy-done.1, bf16[64,256]{1,0:T(8,128)(2,1)S(1)} %bitcast.3, bf16[64,256]{1,0:T(8,128)(2,1)S(1)} %bitcast.4, ...), custom_call_target="tpu_custom_call" | custom-call | flops 1207959552 | bytes 4194304 | tf_op jit(solution)/shard_map/pallas_call | solution.py:173
  (2 shorter events, 0.0 us)
Async XLA Ops:
  1.3 22.1 %all-to-all-start = ((s32[32,1,32]{2,1,0:T(1,128)}), s32[32,1,32]{2,1,0:T(1,128)S(1)}, u32[]{:S(2)}, u32[]{:S(2)}) async-start(s32[32,1,32]{2,1,0:T(1,128)} %broadcast_in_dim.6), calls=%async_computation | async-start | bytes 32768 | tf_op jit(solution)/shard_map/all_to_all | solution.py:155
  14.8 1.6 %copy-start = (bf16[4352,256]{1,0:T(8,128)(2,1)S(1)}, bf16[4352,256]{1,0:T(8,128)(2,1)}, u32[]{:S(2)}) copy-start(bf16[4352,256]{1,0:T(8,128)(2,1)} %w_hbm.1) | copy-start | bytes 6684676
  16.4 1.3 %copy-start.4 = (bf16[4,64,576]{2,1,0:T(8,128)(2,1)S(1)}, bf16[4,64,576]{2,1,0:T(8,128)(2,1)}, u32[]{:S(2)}) copy-start(bf16[4,64,576]{2,1,0:T(8,128)(2,1)} %param.13) | copy-start | bytes 884740
  19.0 4.4 %copy-start.1 = (bf16[4352,256]{1,0:T(8,128)(2,1)S(1)}, bf16[4352,256]{1,0:T(8,128)(2,1)}, u32[]{:S(2)}) copy-start(bf16[4352,256]{1,0:T(8,128)(2,1)} %w2_ref.1) | copy-start | bytes 6684676
  19.0 4.4 %copy-start.2 = (bf16[256,64]{0,1:T(8,128)(2,1)S(1)}, bf16[256,64]{0,1:T(8,128)(2,1)}, u32[]{:S(2)}) copy-start(bf16[256,64]{0,1:T(8,128)(2,1)} %param.11) | copy-start | bytes 98308
  19.1 4.4 %copy-start.3 = (bf16[256,64]{0,1:T(8,128)(2,1)S(1)}, bf16[256,64]{0,1:T(8,128)(2,1)}, u32[]{:S(2)}) copy-start(bf16[256,64]{0,1:T(8,128)(2,1)} %param.12) | copy-start | bytes 98308

commit v4 on v3

--- a/solution.py
+++ b/solution.py
@@ -108,20 +108,29 @@
     def rows_of(plane):
         return pl.ds(plane * CH, CH)
 
-    for plane in range(1, PLANES - 1):
+    def outer_sum(plane):
         for first in range(0, CH, BLOCK):
             block_of = slice(first, first + BLOCK)
             x = (left[block_of, plane : plane + 1] + right[block_of]).astype(bf16)
             x_ref[pl.ds(plane * CH + first, BLOCK), :] = x
             a_ref[pl.ds(plane * CH + first, BLOCK), :] = activate(x, plane)
 
+    for plane in range(1, 5):
+        outer_sum(plane)
+
     def layer(number, low, high, src, dst):
         d = 2**number
         weights = pw_ref[number]
         lanes = lax.broadcasted_iota(jnp.int32, (BLOCK, COLS), 1)
+        def product(plane):
+            stack = [src[rows_of(plane + (t - 1) * d), :] for t in range(3)] + [x_ref[rows_of(plane), :]]
+            return jnp.dot(weights, jnp.concatenate(stack, axis=0), preferred_element_type=f32)
+
+        ready = product(low)
         for plane in range(low, high):
-            stack = [src[rows_of(plane + (t - 1) * d), :] for t in range(3)] + [x_ref[rows_of(plane), :]]
-            y = jnp.dot(weights, jnp.concatenate(stack, axis=0), preferred_element_type=f32)
+            if number == 0 and plane + 3 < PLANES - 1:
+                outer_sum(plane + 3)
+            y, ready = ready, product(plane + 1) if plane + 1 < high else None
             for first in range(0, CH, BLOCK):
                 before, here, after = (y[3 * first + t * BLOCK : 3 * first + (t + 1) * BLOCK] for t in range(3))
                 if dst is None:

time: 34.1 us -> 34 us (level)
  no operation moved by 1% of the time
where the time goes in v4:
time: 34 us; the launch traced here: 33.8 us
  starting transfers between devices  12.8 us (38%)
  Pallas kernels  11.6 us (34%)
  local copies, waits for them, and re-layouts  7.99 us (24%)
  other arithmetic  1.25 us (4%)
    all_to_all x1, starting transfers between devices, local(): every = lax.all_to_all(copies, 'row', 0, 0, tiled=True)  12.8 us
    pallas_call x1, Pallas kernels, local(): pl.pallas_call(pair_kernel, out_shape=jax.ShapeDtypeStruct((CH, ROWS, COL...  10.3 us
    transpose x1, local copies, waits for them, and re-layouts, local(): pair_weights.reshape(LAYERS, blocks, BLOCK, 3, 3, CH)  1.73 us
    unnamed x10, local copies, waits for them, and re-layouts  1.64 us
    reshape x1, local copies, waits for them, and re-layouts, local(): pair_weights.reshape(LAYERS, blocks, BLOCK, 3, 3, CH)  1.34 us
    pallas_call x1, Pallas kernels, local(): pl.pallas_call(tables_kernel, in_specs=[vmem, pl.BlockSpec(memory_space=p...  1.3 us
    broadcast_in_dim x1, local copies, waits for them, and re-layouts, local(): copies = jnp.broadcast_to(residues, (lax.axis_size('row'), 1, ROWS))  1.26 us
    reshape x1, local copies, waits for them, and re-layouts, local(): pw = pw.reshape(LAYERS, 3 * CH, 3 * CH)  1.19 us
  transfers between devices with their start and end apart: 1, of which 1 were waited for; matrix products, arithmetic and copies ran while one was open for 19% of the time, Pallas kernels for 4%

profile of v4, /device:TPU:1, one launch (start us, length us, event | category | flops | bytes accessed | tf_op | source)
XLA Modules:
  0.0 33.8 jit_solution(4733290126040515327)
XLA Ops:
  0.0 1.3 %broadcast_in_dim.6 = s32[32,1,32]{2,1,0:T(1,128)} broadcast(s32[32]{0:T(128)} %param.7), dimensions={2} | broadcast | bytes 4224 | tf_op jit(solution)/shard_map/broadcast_in_dim | solution.py:163
  1.3 12.8 %all-to-all-start = ((s32[32,1,32]{2,1,0:T(1,128)}), s32[32,1,32]{2,1,0:T(1,128)S(1)}, u32[]{:S(2)}, u32[]{:S(2)}) async-start(s32[32,1,32]{2,1,0:T(1,128)} %broadcast_in_dim.6), calls=%async_computation | async-start | bytes 32768 | tf_op jit(solution)/shard_map/all_to_all | solution.py:164
  14.0 0.7 %pad.4.table_ref = bf16[32,256]{1,0:T(8,128)(2,1)S(1)} pad(bf16[21,256]{1,0:T(8,128)(2,1)} %param.8, bf16[]{:T(256)} %constant.5.clone.1), padding=0_11x0_0 | pad | bytes 27138 | tf_op jit(solution)/shard_map/jit(_pad)/pad | solution.py:165
  14.8 0.0 copy-start
  14.8 1.6 %copy-done = bf16[4352,256]{1,0:T(8,128)(2,1)S(1)} copy-done((bf16[4352,256]{1,0:T(8,128)(2,1)S(1)}, bf16[4352,256]{1,0:T(8,128)(2,1)}, u32[]{:S(2)}) %copy-start) | copy-done | bytes 2228248
  16.4 0.0 copy-start.4
  16.4 1.3 %shard_map.73.tt_ref = bf16[256,544]{1,0:T(8,128)(2,1)S(1)} custom-call(bf16[32,256]{1,0:T(8,128)(2,1)S(1)} %pad.4.table_ref, bf16[4352,256]{1,0:T(8,128)(2,1)S(1)} %copy-done), custom_call_target="tpu_custom_call" | custom-call | flops 71303168 | bytes 3145728 | tf_op jit(solution)/shard_map/pallas_call | solution.py:166
  17.7 0.0 copy-done.4
  17.7 1.3 %reshape.27 = bf16[4,4,16,3,3,64]{5,4,3,2,1,0:T(4,128)(2,1)} reshape(bf16[4,64,576]{2,1,0:T(8,128)(2,1)S(1)} %copy-done.4) | data formatting | bytes 589824 | tf_op jit(solution)/shard_map/reshape | solution.py:177
  19.0 0.0 copy-start.1
  19.0 0.0 copy-start.2
  19.1 0.0 copy-start.3
  19.1 1.7 %copy.9 = bf16[4,4,3,16,3,64]{5,4,3,2,1,0:T(4,128)(2,1)S(1)} copy(bf16[4,4,3,16,3,64]{5,2,4,3,1,0:T(4,128)(2,1)} %bitcast.5) | data formatting | bytes 589824 | tf_op jit(solution)/shard_map/transpose | solution.py:177
  20.8 1.2 %reshape.28 = bf16[4,192,192]{2,1,0:T(8,128)(2,1)} reshape(bf16[4,4,3,16,3,64]{5,4,3,2,1,0:T(4,128)(2,1)S(1)} %copy.9) | data formatting | bytes 589824 | tf_op jit(solution)/shard_map/reshape | solution.py:178
  22.0 0.1 add.25
  22.1 0.1 fusion
  22.2 1.1 %pad_maximum_fusion.pw_ref = bf16[4,192,256]{2,1,0:T(8,128)(2,1)S(1)} fusion(bf16[4,192,64]{2,1,0:T(8,128)(2,1)S(1)} %broadcast_in_dim.7, bf16[4,192,192]{2,1,0:T(8,128)(2,1)} %reshape.28), kind=kLoop, calls=%fused_computation | loop fusion | flops 786432 | bytes 786432 | tf_op jit(solution)/shard_map/concatenate | solution.py:181
  23.3 0.1 all-to-all-done.res_ref
  23.4 0.0 copy-done.1
  23.4 0.0 copy-done.2
  23.4 0.0 copy-done.3
  23.4 10.3 %shard_map.74 = bf16[64,32,128]{2,1,0:T(8,128)(2,1)} custom-call(s32[32,1,32]{2,1,0:T(1,128)S(1)} %all-to-all-done.res_ref, bf16[256,544]{1,0:T(8,128)(2,1)S(1)} %shard_map.73.tt_ref, bf16[4352,256]{1,0:T(8,128)(2,1)S(1)} %copy-done.1, bf16[64,256]{1,0:T(8,128)(2,1)S(1)} %bitcast.3, bf16[64,256]{1,0:T(8,128)(2,1)S(1)} %bitcast.4, ...), custom_call_target="tpu_custom_call" | custom-call | flops 1207959552 | bytes 4194304 | tf_op jit(solution)/shard_map/pallas_call | solution.py:182
  (2 shorter events, 0.0 us)
Async XLA Ops:
  1.3 22.1 %all-to-all-start = ((s32[32,1,32]{2,1,0:T(1,128)}), s32[32,1,32]{2,1,0:T(1,128)S(1)}, u32[]{:S(2)}, u32[]{:S(2)}) async-start(s32[32,1,32]{2,1,0:T(1,128)} %broadcast_in_dim.6), calls=%async_computation | async-start | bytes 32768 | tf_op jit(solution)/shard_map/all_to_all | solution.py:164
  14.8 1.6 %copy-start = (bf16[4352,256]{1,0:T(8,128)(2,1)S(1)}, bf16[4352,256]{1,0:T(8,128)(2,1)}, u32[]{:S(2)}) copy-start(bf16[4352,256]{1,0:T(8,128)(2,1)} %w_hbm.1) | copy-start | bytes 6684676
  16.4 1.3 %copy-start.4 = (bf16[4,64,576]{2,1,0:T(8,128)(2,1)S(1)}, bf16[4,64,576]{2,1,0:T(8,128)(2,1)}, u32[]{:S(2)}) copy-start(bf16[4,64,576]{2,1,0:T(8,128)(2,1)} %param.13) | copy-start | bytes 884740
  19.0 4.4 %copy-start.1 = (bf16[4352,256]{1,0:T(8,128)(2,1)S(1)}, bf16[4352,256]{1,0:T(8,128)(2,1)}, u32[]{:S(2)}) copy-start(bf16[4352,256]{1,0:T(8,128)(2,1)} %w2_ref.1) | copy-start | bytes 6684676
  19.0 4.4 %copy-start.2 = (bf16[256,64]{0,1:T(8,128)(2,1)S(1)}, bf16[256,64]{0,1:T(8,128)(2,1)}, u32[]{:S(2)}) copy-start(bf16[256,64]{0,1:T(8,128)(2,1)} %param.11) | copy-start | bytes 98308
  19.1 4.4 %copy-start.3 = (bf16[256,64]{0,1:T(8,128)(2,1)S(1)}, bf16[256,64]{0,1:T(8,128)(2,1)}, u32[]{:S(2)}) copy-start(bf16[256,64]{0,1:T(8,128)(2,1)} %param.12) | copy-start | bytes 98308
